TPU v7x, 32 devices: a whole 2x2x4 slice. The times are simulated.
32 devices in a mesh: wide: 8 (over z, y), narrow: 4 (over x, core).
Axes of the slice: x: 2, y: 2, z: 4, core: 2. Of those that a mesh axis runs over, the one named last changes fastest.
Arguments:
- atm_state: float32 [144, 65536], P(None, ('wide', 'narrow')), may hold values from -6 to 6
- group_owner: int32 [65536, 1], P(('wide', 'narrow')), may hold values from 0 to 31; in each aligned block of 2048 rows (0 to 2047, 2048 to 4095, ...) at most 128 rows name the same one
- regime_ops: bfloat16 [32, 4, 144, 144], P(('wide', 'narrow')), may hold values from -0.5 to 0.5
- flux_map: bfloat16 [144, 4], replicated, may hold values from -0.5 to 0.5
- remap_src: int32 [4, 256, 1024], P(None, 'wide', 'narrow'), may hold values from 0 to 8
- remap_weight: float32 [4, 256, 1024], P(None, 'wide', 'narrow'), may hold values from 0.05 to 0.6
- ocean_mask: int32 [256, 1024], P('wide', 'narrow'), may hold values 0 or 1
- tracer: float32 [62, 256, 1024], P(None, 'wide', 'narrow'), may hold values from -6 to 6
- surface_height: float32 [256, 1024], P('wide', 'narrow'), may hold values from -3 to 3
- transports: float32 [2, 256, 1024], P(None, 'wide', 'narrow'), may hold values from -3 to 3
Outputs:
- atm_new: float32 [144, 65536], P(None, ('wide', 'narrow'))
- tracer_new: float32 [62, 256, 1024], P(None, 'wide', 'narrow')
- height_new: float32 [256, 1024], P('wide', 'narrow')
- transports_new: float32 [2, 256, 1024], P(None, 'wide', 'narrow')
Inputs may be any that keep to these rules, and one draw needn't show every extreme that they name: `group_owner`: among the 2048 columns of one device no owner is named more than 128 times, and one is named exactly 128 times.
All inputs are finite; a program needn't handle non-finite values. No bound on the sum of `ocean_mask` on one device may be relied on, other than what follows from the above.
Results may differ from a plain program's by a relative error of at most 0.0043.
Values may be sent and summed in bfloat16 or wider, within the bound.
A program may use at most 128 MiB of HBM per device.

v0:
```python
import jax
import jax.numpy as jnp
from jax import lax
from jax.sharding import PartitionSpec as P

AC = 128
NSUB = 4


relax_rate = 0.5
kappa_mix = 0.2
heat_gain = 0.5
gravity = 0.7
depth_mean = 0.7
wind_gain = 0.3
fresh_gain = 0.3


def with_halo(cells, sides, width):
    for axis, dim in sides:
        count = lax.axis_size(axis)
        ends = count - 1
        head = lax.slice_in_dim(cells, 0, width, axis=dim)
        tail = lax.slice_in_dim(cells, cells.shape[dim] - width, cells.shape[dim], axis=dim)
        cells = jnp.concatenate(
            [
                lax.ppermute(tail, axis, [(i, (i + 1) % count) for i in range(ends)]),
                cells,
                lax.ppermute(head, axis, [((i + 1) % count, i) for i in range(ends)]),
            ],
            axis=dim,
        )
    return cells


def passed_along(block, axis, distance):
    devices = range(lax.axis_size(axis))
    route = [(i - distance, i) for i in devices if i - distance in devices]
    return lax.ppermute(block, axis, route)


def column_ranks(owners, peers):
    onehot = (owners[:, None] == jnp.arange(peers, dtype=jnp.int32)[None, :]).astype(jnp.int32)
    before = jnp.cumsum(onehot, axis=0) - onehot
    return jnp.sum(before * onehot, axis=1)


def block_width():
    return 512


def place_columns(source, slots, total):
    width = block_width()
    pieces = []
    for start in range(0, total, width):
        selector = (slots[:, None] == (start + jnp.arange(width, dtype=jnp.int32))[None, :]).astype(
            jnp.bfloat16
        )
        pieces.append(
            jnp.dot(source, selector, preferred_element_type=jnp.float32).astype(jnp.bfloat16)
        )
    return jnp.concatenate(pieces, axis=1)


def fetch_columns(source, slots):
    count = slots.shape[0]
    width = block_width()
    lanes = jnp.arange(source.shape[1], dtype=jnp.int32)
    pieces = []
    for start in range(0, count, width):
        wanted = slots[start : start + width]
        selector = (lanes[:, None] == wanted[None, :]).astype(jnp.bfloat16)
        pieces.append(jnp.dot(source, selector, preferred_element_type=jnp.float32))
    return jnp.concatenate(pieces, axis=1)


def physics(operators, columns, flux_map):
    initial = columns.astype(jnp.float32)
    current = initial
    for sweep in range(operators.shape[0]):
        mixed = lax.dot_general(
            operators[sweep],
            current.astype(jnp.bfloat16),
            (((0,), (0,)), ((), ())),
            preferred_element_type=jnp.float32,
        )
        current = current + relax_rate * jnp.tanh(mixed)
    final = current.astype(jnp.bfloat16)
    tendency = (current - initial).astype(jnp.bfloat16)
    fluxes = lax.dot_general(
        flux_map, final, (((0,), (0,)), ((), ())), preferred_element_type=jnp.float32
    ).astype(jnp.bfloat16)
    return (tendency, fluxes)


def diffuse(tracer_ext, mask_ext):
    centre = tracer_ext[:, 1:-1, 1:-1]
    mask_centre = mask_ext[:, 1:-1, 1:-1]
    summed = jnp.zeros_like(centre)
    cuts = (
        (slice(2, None), slice(1, -1)),
        (slice(None, -2), slice(1, -1)),
        (slice(1, -1), slice(2, None)),
        (slice(1, -1), slice(None, -2)),
    )
    for row_cut, col_cut in cuts:
        summed = summed + mask_centre * mask_ext[:, row_cut, col_cut] * (
            tracer_ext[:, row_cut, col_cut] - centre
        )
    return centre + kappa_mix * summed


def momentum(flow, height, height_next, mask, mask_next, stress):
    return mask * mask_next * (flow - gravity * (height_next - height) + wind_gain * stress)


def continuity(height, flow_u, flow_u_west, flow_v, flow_v_south, mask, fresh):
    return mask * (
        height - depth_mean * (flow_u - flow_u_west + (flow_v - flow_v_south)) + fresh_gain * fresh
    )


def per_device(
    atm_state,
    group_owner,
    regime_ops,
    flux_map,
    remap_src,
    remap_weight,
    ocean_mask,
    tracer,
    surface_height,
    transports,
):
    peers = lax.axis_size(("wide", "narrow"))
    wide_count = lax.axis_size("wide")
    narrow_count = lax.axis_size("narrow")
    features = atm_state.shape[0]
    columns_here = atm_state.shape[1]
    nflux = flux_map.shape[1]
    capacity = 2 * columns_here // peers
    total_slots = peers * capacity
    owners = group_owner[:, 0]
    slots = owners * capacity + column_ranks(owners, peers)
    initial = atm_state.astype(jnp.bfloat16)
    outgoing = place_columns(initial, slots, total_slots)
    arrived = lax.all_to_all(outgoing, ("wide", "narrow"), split_axis=1, concat_axis=1, tiled=True)
    tendency, fluxes = physics(regime_ops[0], arrived, flux_map)
    back_tend, back_flux = (
        lax.all_to_all(tendency, ("wide", "narrow"), split_axis=1, concat_axis=1, tiled=True),
        lax.all_to_all(fluxes, ("wide", "narrow"), split_axis=1, concat_axis=1, tiled=True),
    )
    returned = fetch_columns(jnp.concatenate([back_tend, back_flux], axis=0), slots)
    tend_cols = returned[:features]
    flux_cols = returned[features:]
    atm_new = atm_state + tend_cols
    block_rows = columns_here // AC
    flux_block = flux_cols.reshape(nflux, block_rows, AC)
    mask = ocean_mask.astype(jnp.float32)
    flux_ext, tracer_ext, mask_ext = (
        with_halo(flux_block, (("wide", 1), ("narrow", 2)), 1),
        with_halo(tracer, (("wide", 1), ("narrow", 2)), 1),
        with_halo(mask[None], (("wide", 1), ("narrow", 2)), 1),
    )
    my_wide = lax.axis_index("wide")
    my_narrow = lax.axis_index("narrow")
    top_row = jnp.where(my_wide == 0, flux_ext[:, 1:2, :], flux_ext[:, 0:1, :])
    bottom_row = jnp.where(my_wide == wide_count - 1, flux_ext[:, -2:-1, :], flux_ext[:, -1:, :])
    clamped = jnp.concatenate([top_row, flux_ext[:, 1:-1, :], bottom_row], axis=1)
    left_col = jnp.where(my_narrow == 0, clamped[:, :, 1:2], clamped[:, :, 0:1])
    right_col = jnp.where(my_narrow == narrow_count - 1, clamped[:, :, -2:-1], clamped[:, :, -1:])
    clamped = jnp.concatenate([left_col, clamped[:, :, 1:-1], right_col], axis=2)
    ext_rows = block_rows + 2
    ext_cols = AC + 2
    doubled = jnp.broadcast_to(
        clamped[:, :, None, :, None], (nflux, ext_rows, 2, ext_cols, 2)
    ).reshape(nflux, 2 * ext_rows, 2 * ext_cols)
    ocean_rows = remap_src.shape[1]
    ocean_cols = remap_src.shape[2]
    ocean_flux = jnp.zeros((nflux, ocean_rows, ocean_cols), jnp.float32)
    for code in range(9):
        row_off = 2 * (code // 3)
        col_off = 2 * (code % 3)
        weight_sum = jnp.sum(jnp.where(remap_src == code, remap_weight, 0.0), axis=0)
        shifted = doubled[:, row_off : row_off + ocean_rows, col_off : col_off + ocean_cols]
        ocean_flux = ocean_flux + weight_sum[None] * shifted
    tracer_new = diffuse(tracer_ext, mask_ext)
    tracer_new = tracer_new.at[0].add(heat_gain * mask * ocean_flux[0])
    mask_east = mask_ext[0, 1:-1, 2:]
    mask_north = mask_ext[0, 2:, 1:-1]
    height = surface_height
    flow_u = transports[0]
    flow_v = transports[1]
    for substep in range(NSUB):
        north_row = passed_along(height[:1, :], "wide", -1)
        east_column = passed_along(height[:, :1], "narrow", -1)
        height_east = jnp.concatenate([height[:, 1:], east_column], axis=1)
        height_north = jnp.concatenate([height[1:, :], north_row], axis=0)
        flow_u = momentum(flow_u, height, height_east, mask, mask_east, ocean_flux[2])
        flow_v = momentum(flow_v, height, height_north, mask, mask_north, ocean_flux[3])
        west_column = passed_along(flow_u[:, -1:], "narrow", 1)
        south_row = passed_along(flow_v[-1:, :], "wide", 1)
        flow_u_west = jnp.concatenate([west_column, flow_u[:, :-1]], axis=1)
        flow_v_south = jnp.concatenate([south_row, flow_v[:-1, :]], axis=0)
        height = continuity(height, flow_u, flow_u_west, flow_v, flow_v_south, mask, ocean_flux[1])
    return (atm_new, tracer_new, height, jnp.stack([flow_u, flow_v]))


def solution(mesh):
    in_specs = (
        P(None, ("wide", "narrow")),
        P(("wide", "narrow"), None),
        P(("wide", "narrow"), None, None, None),
        P(),
        P(None, "wide", "narrow"),
        P(None, "wide", "narrow"),
        P("wide", "narrow"),
        P(None, "wide", "narrow"),
        P("wide", "narrow"),
        P(None, "wide", "narrow"),
    )
    out_specs = (
        P(None, ("wide", "narrow")),
        P(None, "wide", "narrow"),
        P("wide", "narrow"),
        P(None, "wide", "narrow"),
    )
    return jax.shard_map(
        per_device, mesh=mesh, in_specs=in_specs, out_specs=out_specs, check_vma=False
    )
```

profile of v0, /device:TPU:0, one launch (start us, length us, event | category | flops | bytes accessed | tf_op | source)
XLA Modules:
  0.0 242.8 jit_solution(7221182862590419493)
XLA Ops:
  1.5 9.1 %reduce-window.6 = s32[32,16,128]{2,1,0:T(8,128)S(1)} reduce-window(s32[32,16,128]{2,1,0:T(8,128)S(1)} %fusion.154, s32[]{:T(128)} %constant.63.clone.1), window={size=1x1x128 pad=0_0x0_0x127_0}, to_apply=%region_0.0 | reduce-window | flops 8323072 | bytes 524292 | tf_op jit(solution)/shard_map/reduce-window
  18.9 37.8 %all_to_all.36 = bf16[144,32,128]{2,0,1:T(8,128)(2,1)S(1)} all-to-all(bf16[144,32,128]{2,0,1:T(8,128)(2,1)S(1)} %copy_bitcast_fusion.2), channel_id=1, replica_groups=mesh['wide'=8,'narrow'=4] {'wide','narrow'}, dimensions={1} | all-to-all | bytes 2359296 | tf_op jit(solution)/shard_map/all_to_all | solution.py:147
  58.8 1.3 copy_bitcast_fusion.1
  60.0 2.7 %all-to-all-start.1 = ((bf16[144,32,128]{2,0,1:T(8,128)(2,1)}), bf16[144,32,128]{2,0,1:T(8,128)(2,1)S(1)}, u32[]{:S(2)}, u32[]{:S(2)}) async-start(bf16[144,32,128]{2,0,1:T(8,128)(2,1)} %copy_bitcast_fusion.1), calls=%async_computation.1 | async-start | bytes 2359296 | tf_op jit(solution)/shard_map/all_to_all | solution.py:150
  64.7 1.3 collective-permute-start
  65.9 5.1 %collective-permute-start.2 = (f32[1,1,256]{2,1,0:T(1,128)}, f32[1,1,256]{2,1,0:T(1,128)}, u32[]{:S(2)}, u32[]{:S(2)}) collective-permute-start(f32[1,1,256]{2,1,0:T(1,128)} %get-tuple-element.57), channel_id=1, source_target_pairs={{0,4},{4,8},{8,12},{12,16},{16,20},{20,24},{24,28},{1,5},{5,9},{9,... | collective-permute-start | bytes 3080 | tf_op jit(solution)/shard_map/ppermute | solution.py:27
  71.1 1.3 slice.367
  72.4 1.3 collective-permute-start.12
  73.7 1.2 slice.373
  74.9 1.3 collective-permute-start.14
  76.2 1.9 fusion.226
  78.1 1.3 collective-permute-start.1
  80.7 1.8 select_reduce_fusion.8
  82.5 1.4 slice.366
  83.9 1.4 slice.372
  85.3 1.4 pad_maximum_fusion.16
  87.6 4.6 %all-to-all-done.1 = bf16[144,32,128]{2,0,1:T(8,128)(2,1)S(1)} async-done(((bf16[144,32,128]{2,0,1:T(8,128)(2,1)}), bf16[144,32,128]{2,0,1:T(8,128)(2,1)S(1)}, u32[]{:S(2)}, u32[]{:S(2)}) %all-to-all-start.1) | async-done | bytes 1179680 | tf_op jit(solution)/shard_map/all_to_all | solution.py:150
  92.2 6.3 %all-to-all-start.2 = ((bf16[4,32,128]{2,0,1:T(4,128)(2,1)}), bf16[4,32,128]{2,0,1:T(4,128)(2,1)S(1)}, u32[]{:S(2)}, u32[]{:S(2)}) async-start(bf16[4,32,128]{2,0,1:T(4,128)(2,1)} %fusion.147), calls=%async_computation.2 | async-start | bytes 65536 | tf_op jit(solution)/shard_map/all_to_all | solution.py:151
  98.6 6.9 %all-to-all-done.2 = bf16[4,32,128]{2,0,1:T(4,128)(2,1)S(1)} async-done(((bf16[4,32,128]{2,0,1:T(4,128)(2,1)}), bf16[4,32,128]{2,0,1:T(4,128)(2,1)S(1)}, u32[]{:S(2)}, u32[]{:S(2)}) %all-to-all-start.2) | async-done | bytes 32800 | tf_op jit(solution)/shard_map/all_to_all | solution.py:151
  105.6 1.6 fusion
  107.2 1.6 fusion.1
  108.8 1.6 fusion.2
  110.5 1.6 fusion.3
  112.2 2.5 %collective-permute-start.8 = (f32[4,1,128]{2,1,0:T(1,128)S(1)}, f32[4,1,128]{2,1,0:T(1,128)S(1)}, u32[]{:S(2)}, u32[]{:S(2)}) collective-permute-start(f32[4,1,128]{2,1,0:T(1,128)S(1)} %get-tuple-element.55), channel_id=1, source_target_pairs={{0,4},{4,8},{8,12},{12,16},{16,20},{20,24},{24,28},{1,5},{5,9},{9,... | collective-permute-start | bytes 6152 | tf_op jit(solution)/shard_map/ppermute | solution.py:27
  114.6 1.3 collective-permute-start.9
  116.0 4.5 %collective-permute-start.3 = (f32[62,1,256]{2,1,0:T(1,128)S(1)}, f32[62,1,256]{2,1,0:T(1,128)S(1)}, u32[]{:S(2)}, u32[]{:S(2)}) collective-permute-start(f32[62,1,256]{2,1,0:T(1,128)S(1)} %copy-done.39), channel_id=1, source_target_pairs={{0,4},{4,8},{8,12},{12,16},{16,20},{20,24},{24,28},{1,5},{5,9},{9,... | collective-permute-start | bytes 190472 | tf_op jit(solution)/shard_map/ppermute | solution.py:27
  120.6 1.3 collective-permute-start.4
  122.0 3.0 %collective-permute-start.10 = (f32[4,18,1]{2,1,0:T(8,128)S(1)}, f32[4,18,1]{2,1,0:T(8,128)S(1)}, u32[]{:S(2)}, u32[]{:S(2)}) collective-permute-start(f32[4,18,1]{2,1,0:T(8,128)S(1)} %get-tuple-element.41), channel_id=1, source_target_pairs={{0,1},{1,2},{2,3},{4,5},{5,6},{6,7},{8,9},{9,10},{10,11},{12,13},{... | collective-permute-start | bytes 872 | tf_op jit(solution)/shard_map/ppermute | solution.py:27
  125.1 1.3 collective-permute-start.11
  126.4 1.3 pad_maximum_fusion
  127.7 3.3 %collective-permute-start.6 = (f32[1,34,1]{2,1,0:T(8,128)S(1)}, f32[1,34,1]{2,1,0:T(8,128)S(1)}, u32[]{:S(2)}, u32[]{:S(2)}) collective-permute-start(f32[1,34,1]{2,1,0:T(8,128)S(1)} %get-tuple-element.44), channel_id=1, source_target_pairs={{0,1},{1,2},{2,3},{4,5},{5,6},{6,7},{8,9},{9,10},{10,11},{12,13},{... | collective-permute-start | bytes 416 | tf_op jit(solution)/shard_map/ppermute | solution.py:27
  131.6 1.5 copy.86
  133.1 4.7 %broadcast_in_dim.17 = f32[4,18,2,130,2]{0,4,3,2,1:T(2,128)} broadcast(f32[4,18,130]{0,2,1:T(8,128)} %copy.86), dimensions={0,1,3} | broadcast | bytes 187200 | tf_op jit(solution)/shard_map/broadcast_in_dim | solution.py:175
  137.9 7.1 %reshape.128 = f32[4,36,260]{0,2,1:T(8,128)} reshape(f32[4,18,2,130,2]{0,4,3,2,1:T(2,128)} %broadcast_in_dim.17) | data formatting | bytes 299520 | tf_op jit(solution)/shard_map/reshape | solution.py:177
  145.0 18.1 %fusion.19 = f32[4,32,256]{0,2,1:T(8,128)S(1)} fusion(f32[4,36,260]{0,2,1:T(8,128)} %reshape.128, f32[32,256]{1,0:T(8,128)S(1)} %copy-done.35, f32[32,256]{1,0:T(8,128)S(1)} %copy-done.36, f32[32,256]{1,0:T(8,128)S(1)} %copy-done.29, f32[32,256]{1,0:T(8,128)S(1)} %copy-done.30, f32[32,256]{1,0:T(8,128)S(1)} %copy-done.31, f32[32,256]{1,0:T(8,128)S(1)} %copy-done.32, ...), kind=kLoop, calls=%fused_computation.33 | loop fusion | flops 557056 | bytes 1605632 | tf_op jit(solution)/shard_map/add | solution.py:186
  163.2 8.4 %fusion.17 = (f32[32,256]{1,0:T(8,128)S(1)}, f32[32,256]{1,0:T(8,128)S(1)}, f32[32,256]{1,0:T(8,128)S(1)}, f32[32,256]{1,0:T(8,128)}) fusion(f32[4,32,256]{0,2,1:T(8,128)S(1)} %fusion.19), kind=kLoop, calls=%fused_computation.28 | loop fusion | flops 24576 | bytes 262144 | tf_op jit(solution)/shard_map/mul | solution.py:114
  171.7 1.4 fusion.184
  173.1 4.3 %collective-permute-start.15 = (f32[1,256]{1,0:T(1,128)S(1)}, f32[1,256]{1,0:T(1,128)S(1)}, u32[]{:S(2)}, u32[]{:S(2)}) collective-permute-start(f32[1,256]{1,0:T(1,128)S(1)} %slice.440), channel_id=1, source_target_pairs={{0,4},{4,8},{8,12},{12,16},{16,20},{20,24},{24,28},{1,5},{5,9},{9,... | collective-permute-start | bytes 3080 | tf_op jit(solution)/shard_map/ppermute | solution.py:39
  177.4 1.9 fusion.225
  179.3 1.8 copy.82
  181.1 1.3 collective-permute-start.5
  182.5 3.6 %collective-permute-start.13 = (f32[32,1]{1,0:T(8,128)S(1)}, f32[32,1]{1,0:T(8,128)S(1)}, u32[]{:S(2)}, u32[]{:S(2)}) collective-permute-start(f32[32,1]{1,0:T(8,128)S(1)} %slice.437), channel_id=1, source_target_pairs={{0,1},{1,2},{2,3},{4,5},{5,6},{6,7},{8,9},{9,10},{10,11},{12,13},{... | collective-permute-start | bytes 392 | tf_op jit(solution)/shard_map/ppermute | solution.py:39
  186.1 1.1 copy.84
  187.2 4.4 %collective-permute-start.7 = (f32[62,34,1]{0,2,1:T(1,128)}, f32[62,34,1]{0,2,1:T(1,128)}, u32[]{:S(2)}, u32[]{:S(2)}) collective-permute-start(f32[62,34,1]{0,2,1:T(1,128)} %copy.84), channel_id=1, source_target_pairs={{0,1},{1,2},{2,3},{4,5},{5,6},{6,7},{8,9},{9,10},{10,11},{12,13},{... | collective-permute-start | bytes 25304 | tf_op jit(solution)/shard_map/ppermute | solution.py:27
  192.2 1.3 collective-permute-start.18
  193.5 1.5 multiply_bitcast_fusion
  195.5 2.3 copy.85
  197.8 1.3 collective-permute-start.16
  199.2 1.7 collective-permute-done.16
  201.8 3.3 %collective-permute-start.17 = (f32[32,1]{1,0:T(8,128)S(1)}, f32[32,1]{1,0:T(8,128)S(1)}, u32[]{:S(2)}, u32[]{:S(2)}) collective-permute-start(f32[32,1]{1,0:T(8,128)S(1)} %slice.445), channel_id=1, source_target_pairs={{0,1},{1,2},{2,3},{4,5},{5,6},{6,7},{8,9},{9,10},{10,11},{12,13},{... | collective-permute-start | bytes 392 | tf_op jit(solution)/shard_map/ppermute | solution.py:39
  205.2 4.3 %collective-permute-start.19 = (f32[1,256]{1,0:T(1,128)S(1)}, f32[1,256]{1,0:T(1,128)S(1)}, u32[]{:S(2)}, u32[]{:S(2)}) collective-permute-start(f32[1,256]{1,0:T(1,128)S(1)} %slice.449), channel_id=1, source_target_pairs={{0,4},{4,8},{8,12},{12,16},{16,20},{20,24},{24,28},{1,5},{5,9},{9,... | collective-permute-start | bytes 3080 | tf_op jit(solution)/shard_map/ppermute | solution.py:39
  209.5 4.2 %fusion.66 = f32[62,32,256]{2,1,0:T(8,128)S(1)} fusion(f32[62,32,256]{2,1,0:T(8,128)S(1)} %copy-done.2, f32[62,34,1]{2,1,0:T(8,128)} %copy.85, f32[62,1,256]{2,1,0:T(1,128)} %collective-permute-done.1, f32[62,1,256]{2,1,0:T(1,128)} %copy-done.21, f32[62,34,1]{2,1,0:T(8,128)S(1)} %copy.83, f32[32,256]{1,0:T(8,128)} %get-tuple-element.46, ...), kind=kLoop, calls=%fused_computation.92 | loop fusion | flops 10665984 | bytes 4338144 | tf_op jit(solution)/shard_map/add | solution.py:110
  213.9 1.4 collective-permute-start.22
  215.5 1.3 collective-permute-start.20
  216.9 1.7 collective-permute-done.20
  219.6 2.7 %collective-permute-start.21 = (f32[32,1]{1,0:T(8,128)S(1)}, f32[32,1]{1,0:T(8,128)S(1)}, u32[]{:S(2)}, u32[]{:S(2)}) collective-permute-start(f32[32,1]{1,0:T(8,128)S(1)} %slice.453), channel_id=1, source_target_pairs={{0,1},{1,2},{2,3},{4,5},{5,6},{6,7},{8,9},{9,10},{10,11},{12,13},{... | collective-permute-start | bytes 392 | tf_op jit(solution)/shard_map/ppermute | solution.py:39
  222.4 4.3 %collective-permute-start.23 = (f32[1,256]{1,0:T(1,128)S(1)}, f32[1,256]{1,0:T(1,128)S(1)}, u32[]{:S(2)}, u32[]{:S(2)}) collective-permute-start(f32[1,256]{1,0:T(1,128)S(1)} %slice.457), channel_id=1, source_target_pairs={{0,4},{4,8},{8,12},{12,16},{16,20},{20,24},{24,28},{1,5},{5,9},{9,... | collective-permute-start | bytes 3080 | tf_op jit(solution)/shard_map/ppermute | solution.py:39
  226.6 1.1 slice_add_fusion
  228.0 1.3 collective-permute-start.26
  229.4 1.3 collective-permute-start.24
  230.8 1.7 collective-permute-done.24
  232.4 1.3 collective-permute-done.26
  233.9 2.2 collective-permute-start.25
  236.1 4.7 %collective-permute-start.27 = (f32[1,256]{1,0:T(1,128)S(1)}, f32[1,256]{1,0:T(1,128)S(1)}, u32[]{:S(2)}, u32[]{:S(2)}) collective-permute-start(f32[1,256]{1,0:T(1,128)S(1)} %slice.465), channel_id=1, source_target_pairs={{0,4},{4,8},{8,12},{12,16},{16,20},{20,24},{24,28},{1,5},{5,9},{9,... | collective-permute-start | bytes 3080 | tf_op jit(solution)/shard_map/ppermute | solution.py:39
  (191 shorter events, 22.4 us)
Async XLA Ops:
  0.6 86.1 %copy-start = (bf16[144,4]{0,1:T(4,128)(2,1)S(1)}, bf16[144,4]{0,1:T(4,128)(2,1)}, u32[]{:S(2)}) copy-start(bf16[144,4]{0,1:T(4,128)(2,1)} %param.15) | copy-start | bytes 3460
  0.6 10.7 %copy-start.27 = (s32[2048,1]{0,1:T(1,128)S(1)}, s32[2048,1]{0,1:T(1,128)}, u32[]{:S(2)}) copy-start(s32[2048,1]{0,1:T(1,128)} %param.13) | copy-start | bytes 24580
  0.7 10.8 %copy-start.4 = (f32[144,2048]{1,0:T(8,128)S(1)}, f32[144,2048]{1,0:T(8,128)}, u32[]{:S(2)}) copy-start(f32[144,2048]{1,0:T(8,128)} %param.12) | copy-start | bytes 3538948
  18.6 38.0 %copy-start.22 = (bf16[1,4,144,144]{3,2,1,0:T(8,128)(2,1)S(1)}, bf16[1,4,144,144]{3,2,1,0:T(8,128)(2,1)}, u32[]{:S(2)}) copy-start(bf16[1,4,144,144]{3,2,1,0:T(8,128)(2,1)} %param.14) | copy-start | bytes 497668
  60.0 32.2 %all-to-all-start.1 = ((bf16[144,32,128]{2,0,1:T(8,128)(2,1)}), bf16[144,32,128]{2,0,1:T(8,128)(2,1)S(1)}, u32[]{:S(2)}, u32[]{:S(2)}) async-start(bf16[144,32,128]{2,0,1:T(8,128)(2,1)} %copy_bitcast_fusion.1), calls=%async_computation.1 | async-start | bytes 2359296 | tf_op jit(solution)/shard_map/all_to_all | solution.py:150
  64.7 20.7 %collective-permute-start = (f32[1,1,256]{2,1,0:T(1,128)}, f32[1,1,256]{2,1,0:T(1,128)S(1)}, u32[]{:S(2)}, u32[]{:S(2)}) collective-permute-start(f32[1,1,256]{2,1,0:T(1,128)} %get-tuple-element.58), channel_id=1, source_target_pairs={{4,0},{8,4},{12,8},{16,12},{20,16},{24,20},{28,24},{5,1},{9,5},{13... | collective-permute-start | bytes 3080 | tf_op jit(solution)/shard_map/ppermute | solution.py:29
  65.9 19.4 %collective-permute-start.2 = (f32[1,1,256]{2,1,0:T(1,128)}, f32[1,1,256]{2,1,0:T(1,128)}, u32[]{:S(2)}, u32[]{:S(2)}) collective-permute-start(f32[1,1,256]{2,1,0:T(1,128)} %get-tuple-element.57), channel_id=1, source_target_pairs={{0,4},{4,8},{8,12},{12,16},{16,20},{20,24},{24,28},{1,5},{5,9},{9,... | collective-permute-start | bytes 3080 | tf_op jit(solution)/shard_map/ppermute | solution.py:27
  72.4 99.2 %collective-permute-start.12 = (f32[32,1]{1,0:T(8,128)}, f32[32,1]{1,0:T(8,128)}, u32[]{:S(2)}, u32[]{:S(2)}) collective-permute-start(f32[32,1]{1,0:T(8,128)} %slice.367), channel_id=1, source_target_pairs={{1,0},{2,1},{3,2},{5,4},{6,5},{7,6},{9,8},{10,9},{11,10},{13,12},{... | collective-permute-start | bytes 392 | tf_op jit(solution)/shard_map/ppermute | solution.py:39
  74.9 96.7 %collective-permute-start.14 = (f32[1,256]{1,0:T(1,128)}, f32[1,256]{1,0:T(1,128)}, u32[]{:S(2)}, u32[]{:S(2)}) collective-permute-start(f32[1,256]{1,0:T(1,128)} %slice.373), channel_id=1, source_target_pairs={{4,0},{8,4},{12,8},{16,12},{20,16},{24,20},{28,24},{5,1},{9,5},{13... | collective-permute-start | bytes 3080 | tf_op jit(solution)/shard_map/ppermute | solution.py:39
  78.1 43.9 %collective-permute-start.1 = (f32[62,1,256]{2,1,0:T(1,128)}, f32[62,1,256]{2,1,0:T(1,128)}, u32[]{:S(2)}, u32[]{:S(2)}) collective-permute-start(f32[62,1,256]{2,1,0:T(1,128)} %get-tuple-element.36), channel_id=1, source_target_pairs={{4,0},{8,4},{12,8},{16,12},{20,16},{24,20},{28,24},{5,1},{9,5},{13... | collective-permute-start | bytes 190472 | tf_op jit(solution)/shard_map/ppermute | solution.py:29
  85.3 86.3 %copy-start.40 = (f32[1,1,256]{2,1,0:T(1,128)}, f32[1,1,256]{2,1,0:T(1,128)S(1)}, u32[]{:S(2)}) copy-start(f32[1,1,256]{2,1,0:T(1,128)S(1)} %collective-permute-done) | copy-start | bytes 3076
  87.6 18.0 %copy-start.43 = (s32[512]{0:T(512)S(1)}, s32[512]{0:T(512)}, u32[]{:S(2)}) copy-start(s32[512]{0:T(512)} %get-tuple-element.59) | copy-start | bytes 6148
  92.2 13.3 %all-to-all-start.2 = ((bf16[4,32,128]{2,0,1:T(4,128)(2,1)}), bf16[4,32,128]{2,0,1:T(4,128)(2,1)S(1)}, u32[]{:S(2)}, u32[]{:S(2)}) async-start(bf16[4,32,128]{2,0,1:T(4,128)(2,1)} %fusion.147), calls=%async_computation.2 | async-start | bytes 65536 | tf_op jit(solution)/shard_map/all_to_all | solution.py:151
  110.5 15.9 %copy-start.1 = (f32[62,32,256]{2,1,0:T(8,128)S(1)}, f32[62,32,256]{2,1,0:T(8,128)}, u32[]{:S(2)}) copy-start(f32[62,32,256]{2,1,0:T(8,128)} %param.19) | copy-start | bytes 6094852
  112.1 15.5 %copy-start.14 = (f32[148,512]{1,0:T(8,128)}, f32[148,512]{1,0:T(8,128)S(1)}, u32[]{:S(2)}) copy-start(f32[148,512]{1,0:T(8,128)S(1)} %fusion.3) | copy-start | bytes 909316
  112.2 3.9 %collective-permute-start.8 = (f32[4,1,128]{2,1,0:T(1,128)S(1)}, f32[4,1,128]{2,1,0:T(1,128)S(1)}, u32[]{:S(2)}, u32[]{:S(2)}) collective-permute-start(f32[4,1,128]{2,1,0:T(1,128)S(1)} %get-tuple-element.55), channel_id=1, source_target_pairs={{0,4},{4,8},{8,12},{12,16},{16,20},{20,24},{24,28},{1,5},{5,9},{9,... | collective-permute-start | bytes 6152 | tf_op jit(solution)/shard_map/ppermute | solution.py:27
  114.6 5.9 %collective-permute-start.9 = (f32[4,1,128]{2,1,0:T(1,128)S(1)}, f32[4,1,128]{2,1,0:T(1,128)S(1)}, u32[]{:S(2)}, u32[]{:S(2)}) collective-permute-start(f32[4,1,128]{2,1,0:T(1,128)S(1)} %get-tuple-element.56), channel_id=1, source_target_pairs={{4,0},{8,4},{12,8},{16,12},{20,16},{24,20},{28,24},{5,1},{9,5},{13... | collective-permute-start | bytes 6152 | tf_op jit(solution)/shard_map/ppermute | solution.py:29
  116.0 9.0 %collective-permute-start.3 = (f32[62,1,256]{2,1,0:T(1,128)S(1)}, f32[62,1,256]{2,1,0:T(1,128)S(1)}, u32[]{:S(2)}, u32[]{:S(2)}) collective-permute-start(f32[62,1,256]{2,1,0:T(1,128)S(1)} %copy-done.39), channel_id=1, source_target_pairs={{0,4},{4,8},{8,12},{12,16},{16,20},{20,24},{24,28},{1,5},{5,9},{9,... | collective-permute-start | bytes 190472 | tf_op jit(solution)/shard_map/ppermute | solution.py:27
  120.6 51.0 %collective-permute-start.4 = (f32[1,34,1]{2,1,0:T(8,128)S(1)}, f32[1,34,1]{2,1,0:T(8,128)S(1)}, u32[]{:S(2)}, u32[]{:S(2)}) collective-permute-start(f32[1,34,1]{2,1,0:T(8,128)S(1)} %get-tuple-element.43), channel_id=1, source_target_pairs={{1,0},{2,1},{3,2},{5,4},{6,5},{7,6},{9,8},{10,9},{11,10},{13,12},{... | collective-permute-start | bytes 416 | tf_op jit(solution)/shard_map/ppermute | solution.py:29
  122.0 5.7 %collective-permute-start.10 = (f32[4,18,1]{2,1,0:T(8,128)S(1)}, f32[4,18,1]{2,1,0:T(8,128)S(1)}, u32[]{:S(2)}, u32[]{:S(2)}) collective-permute-start(f32[4,18,1]{2,1,0:T(8,128)S(1)} %get-tuple-element.41), channel_id=1, source_target_pairs={{0,1},{1,2},{2,3},{4,5},{5,6},{6,7},{8,9},{9,10},{10,11},{12,13},{... | collective-permute-start | bytes 872 | tf_op jit(solution)/shard_map/ppermute | solution.py:27
  125.1 5.9 %collective-permute-start.11 = (f32[4,18,1]{2,1,0:T(8,128)S(1)}, f32[4,18,1]{2,1,0:T(8,128)S(1)}, u32[]{:S(2)}, u32[]{:S(2)}) collective-permute-start(f32[4,18,1]{2,1,0:T(8,128)S(1)} %get-tuple-element.42), channel_id=1, source_target_pairs={{1,0},{2,1},{3,2},{5,4},{6,5},{7,6},{9,8},{10,9},{11,10},{13,12},{... | collective-permute-start | bytes 872 | tf_op jit(solution)/shard_map/ppermute | solution.py:29
  127.7 65.8 %collective-permute-start.6 = (f32[1,34,1]{2,1,0:T(8,128)S(1)}, f32[1,34,1]{2,1,0:T(8,128)S(1)}, u32[]{:S(2)}, u32[]{:S(2)}) collective-permute-start(f32[1,34,1]{2,1,0:T(8,128)S(1)} %get-tuple-element.44), channel_id=1, source_target_pairs={{0,1},{1,2},{2,3},{4,5},{5,6},{6,7},{8,9},{9,10},{10,11},{12,13},{... | collective-permute-start | bytes 416 | tf_op jit(solution)/shard_map/ppermute | solution.py:27
  137.8 7.1 %copy-start.28 = (f32[32,256]{1,0:T(8,128)S(1)}, f32[32,256]{1,0:T(8,128)}, u32[]{:S(2)}) copy-start(f32[32,256]{1,0:T(8,128)} %get-tuple-element.20) | copy-start | bytes 98308
  137.8 7.1 %copy-start.29 = (f32[32,256]{1,0:T(8,128)S(1)}, f32[32,256]{1,0:T(8,128)}, u32[]{:S(2)}) copy-start(f32[32,256]{1,0:T(8,128)} %get-tuple-element.21) | copy-start | bytes 98308
  137.8 7.1 %copy-start.30 = (f32[32,256]{1,0:T(8,128)S(1)}, f32[32,256]{1,0:T(8,128)}, u32[]{:S(2)}) copy-start(f32[32,256]{1,0:T(8,128)} %get-tuple-element.22) | copy-start | bytes 98308
  137.8 7.1 %copy-start.31 = (f32[32,256]{1,0:T(8,128)S(1)}, f32[32,256]{1,0:T(8,128)}, u32[]{:S(2)}) copy-start(f32[32,256]{1,0:T(8,128)} %get-tuple-element.23) | copy-start | bytes 98308
  137.8 7.1 %copy-start.32 = (f32[32,256]{1,0:T(8,128)S(1)}, f32[32,256]{1,0:T(8,128)}, u32[]{:S(2)}) copy-start(f32[32,256]{1,0:T(8,128)} %get-tuple-element.24) | copy-start | bytes 98308
  137.9 7.1 %copy-start.33 = (f32[32,256]{1,0:T(8,128)S(1)}, f32[32,256]{1,0:T(8,128)}, u32[]{:S(2)}) copy-start(f32[32,256]{1,0:T(8,128)} %get-tuple-element.25) | copy-start | bytes 98308
  137.9 7.1 %copy-start.34 = (f32[32,256]{1,0:T(8,128)S(1)}, f32[32,256]{1,0:T(8,128)}, u32[]{:S(2)}) copy-start(f32[32,256]{1,0:T(8,128)} %get-tuple-element.26) | copy-start | bytes 98308
  137.9 7.1 %copy-start.35 = (f32[32,256]{1,0:T(8,128)S(1)}, f32[32,256]{1,0:T(8,128)}, u32[]{:S(2)}) copy-start(f32[32,256]{1,0:T(8,128)} %get-tuple-element.27) | copy-start | bytes 98308
  137.9 7.1 %copy-start.36 = (f32[32,256]{1,0:T(8,128)S(1)}, f32[32,256]{1,0:T(8,128)}, u32[]{:S(2)}) copy-start(f32[32,256]{1,0:T(8,128)} %get-tuple-element.28) | copy-start | bytes 98308
  163.2 8.5 %copy-start.7 = (s32[32,256]{1,0:T(8,128)S(1)}, s32[32,256]{1,0:T(8,128)}, u32[]{:S(2)}) copy-start(s32[32,256]{1,0:T(8,128)} %param.18) | copy-start | bytes 98308
  163.2 8.5 %copy-start.16 = (f32[32,256]{1,0:T(8,128)S(1)}, f32[32,256]{1,0:T(8,128)}, u32[]{:S(2)}) copy-start(f32[32,256]{1,0:T(8,128)} %param.20) | copy-start | bytes 98308
  163.2 8.5 %copy-start.18 = (f32[1,32,256]{2,1,0:T(8,128)S(1)}, f32[1,32,256]{2,1,0:T(8,128)}, u32[]{:S(2)}) copy-start(f32[1,32,256]{2,1,0:T(8,128)} %copy-done.17) | copy-start | bytes 98308
  163.2 8.5 %copy-start.25 = (f32[32,255]{1,0:T(8,128)S(1)}, f32[32,255]{1,0:T(8,128)}, u32[]{:S(2)}) copy-start(f32[32,255]{1,0:T(8,128)} %slice.366) | copy-start | bytes 97924
  163.2 8.5 %copy-start.26 = (f32[31,256]{1,0:T(8,128)S(1)}, f32[31,256]{1,0:T(8,128)}, u32[]{:S(2)}) copy-start(f32[31,256]{1,0:T(8,128)} %slice.372) | copy-start | bytes 95236
  163.2 8.5 %copy-start.38 = (f32[2,32,256]{2,1,0:T(8,128)S(1)}, f32[2,32,256]{2,1,0:T(8,128)}, u32[]{:S(2)}) copy-start(f32[2,32,256]{2,1,0:T(8,128)} %param.21) | copy-start | bytes 196612
  173.1 18.4 %collective-permute-start.15 = (f32[1,256]{1,0:T(1,128)S(1)}, f32[1,256]{1,0:T(1,128)S(1)}, u32[]{:S(2)}, u32[]{:S(2)}) collective-permute-start(f32[1,256]{1,0:T(1,128)S(1)} %slice.440), channel_id=1, source_target_pairs={{0,4},{4,8},{8,12},{12,16},{16,20},{20,24},{24,28},{1,5},{5,9},{9,... | collective-permute-start | bytes 3080 | tf_op jit(solution)/shard_map/ppermute | solution.py:39
  179.3 6.8 %copy-start.3 = (f32[62,34,1]{2,1,0:T(8,128)S(1)}, f32[62,34,1]{2,1,0:T(8,128)}, u32[]{:S(2)}) copy-start(f32[62,34,1]{2,1,0:T(8,128)} %get-tuple-element.34) | copy-start | bytes 25300
  179.3 14.2 %copy-start.41 = (f32[1,1,256]{2,1,0:T(1,128)S(1)}, f32[1,1,256]{2,1,0:T(1,128)}, u32[]{:S(2)}) copy-start(f32[1,1,256]{2,1,0:T(1,128)} %copy-done.40) | copy-start | bytes 3076
  181.1 13.9 %collective-permute-start.5 = (f32[62,34,1]{0,2,1:T(1,128)S(1)}, f32[62,34,1]{0,2,1:T(1,128)S(1)}, u32[]{:S(2)}, u32[]{:S(2)}) collective-permute-start(f32[62,34,1]{0,2,1:T(1,128)S(1)} %copy.82), channel_id=1, source_target_pairs={{1,0},{2,1},{3,2},{5,4},{6,5},{7,6},{9,8},{10,9},{11,10},{13,12},{... | collective-permute-start | bytes 25304 | tf_op jit(solution)/shard_map/ppermute | solution.py:29
  182.5 9.0 %collective-permute-start.13 = (f32[32,1]{1,0:T(8,128)S(1)}, f32[32,1]{1,0:T(8,128)S(1)}, u32[]{:S(2)}, u32[]{:S(2)}) collective-permute-start(f32[32,1]{1,0:T(8,128)S(1)} %slice.437), channel_id=1, source_target_pairs={{0,1},{1,2},{2,3},{4,5},{5,6},{6,7},{8,9},{9,10},{10,11},{12,13},{... | collective-permute-start | bytes 392 | tf_op jit(solution)/shard_map/ppermute | solution.py:39
  187.2 22.3 %copy-start.2 = (f32[62,32,256]{2,1,0:T(8,128)S(1)}, f32[62,32,256]{2,1,0:T(8,128)}, u32[]{:S(2)}) copy-start(f32[62,32,256]{2,1,0:T(8,128)} %param.19) | copy-start | bytes 6094852
  187.2 8.4 %collective-permute-start.7 = (f32[62,34,1]{0,2,1:T(1,128)}, f32[62,34,1]{0,2,1:T(1,128)}, u32[]{:S(2)}, u32[]{:S(2)}) collective-permute-start(f32[62,34,1]{0,2,1:T(1,128)} %copy.84), channel_id=1, source_target_pairs={{0,1},{1,2},{2,3},{4,5},{5,6},{6,7},{8,9},{9,10},{10,11},{12,13},{... | collective-permute-start | bytes 25304 | tf_op jit(solution)/shard_map/ppermute | solution.py:27
  192.2 8.8 %collective-permute-start.18 = (f32[1,256]{1,0:T(1,128)}, f32[1,256]{1,0:T(1,128)}, u32[]{:S(2)}, u32[]{:S(2)}) collective-permute-start(f32[1,256]{1,0:T(1,128)} %slice.448), channel_id=1, source_target_pairs={{4,0},{8,4},{12,8},{16,12},{20,16},{24,20},{28,24},{5,1},{9,5},{13... | collective-permute-start | bytes 3080 | tf_op jit(solution)/shard_map/ppermute | solution.py:39
  197.8 3.1 %collective-permute-start.16 = (f32[32,1]{1,0:T(8,128)S(1)}, f32[32,1]{1,0:T(8,128)S(1)}, u32[]{:S(2)}, u32[]{:S(2)}) collective-permute-start(f32[32,1]{1,0:T(8,128)S(1)} %slice.444), channel_id=1, source_target_pairs={{1,0},{2,1},{3,2},{5,4},{6,5},{7,6},{9,8},{10,9},{11,10},{13,12},{... | collective-permute-start | bytes 392 | tf_op jit(solution)/shard_map/ppermute | solution.py:39
  201.8 11.9 %collective-permute-start.17 = (f32[32,1]{1,0:T(8,128)S(1)}, f32[32,1]{1,0:T(8,128)S(1)}, u32[]{:S(2)}, u32[]{:S(2)}) collective-permute-start(f32[32,1]{1,0:T(8,128)S(1)} %slice.445), channel_id=1, source_target_pairs={{0,1},{1,2},{2,3},{4,5},{5,6},{6,7},{8,9},{9,10},{10,11},{12,13},{... | collective-permute-start | bytes 392 | tf_op jit(solution)/shard_map/ppermute | solution.py:39
  205.2 8.6 %collective-permute-start.19 = (f32[1,256]{1,0:T(1,128)S(1)}, f32[1,256]{1,0:T(1,128)S(1)}, u32[]{:S(2)}, u32[]{:S(2)}) collective-permute-start(f32[1,256]{1,0:T(1,128)S(1)} %slice.449), channel_id=1, source_target_pairs={{0,4},{4,8},{8,12},{12,16},{16,20},{20,24},{24,28},{1,5},{5,9},{9,... | collective-permute-start | bytes 3080 | tf_op jit(solution)/shard_map/ppermute | solution.py:39
  209.5 5.8 %copy-start.9 = (f32[148,512]{1,0:T(8,128)S(1)}, f32[148,512]{1,0:T(8,128)}, u32[]{:S(2)}) copy-start(f32[148,512]{1,0:T(8,128)} %copy-done.8) | copy-start | bytes 909316
  209.5 5.8 %copy-start.11 = (f32[148,512]{1,0:T(8,128)S(1)}, f32[148,512]{1,0:T(8,128)}, u32[]{:S(2)}) copy-start(f32[148,512]{1,0:T(8,128)} %copy-done.10) | copy-start | bytes 909316
  209.5 5.8 %copy-start.13 = (f32[148,512]{1,0:T(8,128)S(1)}, f32[148,512]{1,0:T(8,128)}, u32[]{:S(2)}) copy-start(f32[148,512]{1,0:T(8,128)} %copy-done.12) | copy-start | bytes 909316
  209.5 5.8 %copy-start.15 = (f32[148,512]{1,0:T(8,128)S(1)}, f32[148,512]{1,0:T(8,128)}, u32[]{:S(2)}) copy-start(f32[148,512]{1,0:T(8,128)} %copy-done.14) | copy-start | bytes 909316
  213.7 5.8 %copy-start.19 = (f32[32,256]{1,0:T(8,128)S(1)}, f32[32,256]{1,0:T(8,128)}, u32[]{:S(2)}) copy-start(f32[32,256]{1,0:T(8,128)} %get-tuple-element.30) | copy-start | bytes 98308
  213.7 12.9 %copy-start.5 = (f32[144,2048]{1,0:T(8,128)S(1)}, f32[144,2048]{1,0:T(8,128)}, u32[]{:S(2)}) copy-start(f32[144,2048]{1,0:T(8,128)} %param.12) | copy-start | bytes 3538948
  213.9 5.6 %collective-permute-start.22 = (f32[1,256]{1,0:T(1,128)S(1)}, f32[1,256]{1,0:T(1,128)S(1)}, u32[]{:S(2)}, u32[]{:S(2)}) collective-permute-start(f32[1,256]{1,0:T(1,128)S(1)} %slice.456), channel_id=1, source_target_pairs={{4,0},{8,4},{12,8},{16,12},{20,16},{24,20},{28,24},{5,1},{9,5},{13... | collective-permute-start | bytes 3080 | tf_op jit(solution)/shard_map/ppermute | solution.py:39
  215.5 3.1 %collective-permute-start.20 = (f32[32,1]{1,0:T(8,128)S(1)}, f32[32,1]{1,0:T(8,128)S(1)}, u32[]{:S(2)}, u32[]{:S(2)}) collective-permute-start(f32[32,1]{1,0:T(8,128)S(1)} %slice.452), channel_id=1, source_target_pairs={{1,0},{2,1},{3,2},{5,4},{6,5},{7,6},{9,8},{10,9},{11,10},{13,12},{... | collective-permute-start | bytes 392 | tf_op jit(solution)/shard_map/ppermute | solution.py:39
  216.8 12.5 %copy-start.24 = (f32[32,256]{1,0:T(8,128)S(1)}, f32[32,256]{1,0:T(8,128)}, u32[]{:S(2)}) copy-start(f32[32,256]{1,0:T(8,128)} %get-tuple-element.19) | copy-start | bytes 98308
  219.6 8.1 %collective-permute-start.21 = (f32[32,1]{1,0:T(8,128)S(1)}, f32[32,1]{1,0:T(8,128)S(1)}, u32[]{:S(2)}, u32[]{:S(2)}) collective-permute-start(f32[32,1]{1,0:T(8,128)S(1)} %slice.453), channel_id=1, source_target_pairs={{0,1},{1,2},{2,3},{4,5},{5,6},{6,7},{8,9},{9,10},{10,11},{12,13},{... | collective-permute-start | bytes 392 | tf_op jit(solution)/shard_map/ppermute | solution.py:39
  222.4 5.6 %collective-permute-start.23 = (f32[1,256]{1,0:T(1,128)S(1)}, f32[1,256]{1,0:T(1,128)S(1)}, u32[]{:S(2)}, u32[]{:S(2)}) collective-permute-start(f32[1,256]{1,0:T(1,128)S(1)} %slice.457), channel_id=1, source_target_pairs={{0,4},{4,8},{8,12},{12,16},{16,20},{20,24},{24,28},{1,5},{5,9},{9,... | collective-permute-start | bytes 3080 | tf_op jit(solution)/shard_map/ppermute | solution.py:39
  228.0 5.7 %collective-permute-start.26 = (f32[1,256]{1,0:T(1,128)S(1)}, f32[1,256]{1,0:T(1,128)S(1)}, u32[]{:S(2)}, u32[]{:S(2)}) collective-permute-start(f32[1,256]{1,0:T(1,128)S(1)} %slice.464), channel_id=1, source_target_pairs={{4,0},{8,4},{12,8},{16,12},{20,16},{24,20},{28,24},{5,1},{9,5},{13... | collective-permute-start | bytes 3080 | tf_op jit(solution)/shard_map/ppermute | solution.py:39
  229.3 13.5 %copy-start.6 = (f32[62,32,256]{2,1,0:T(8,128)}, f32[62,32,256]{2,1,0:T(8,128)S(1)}, u32[]{:S(2)}) copy-start(f32[62,32,256]{2,1,0:T(8,128)S(1)} %fusion.163) | copy-start | bytes 6094852
  229.4 3.1 %collective-permute-start.24 = (f32[32,1]{1,0:T(8,128)S(1)}, f32[32,1]{1,0:T(8,128)S(1)}, u32[]{:S(2)}, u32[]{:S(2)}) collective-permute-start(f32[32,1]{1,0:T(8,128)S(1)} %slice.460), channel_id=1, source_target_pairs={{1,0},{2,1},{3,2},{5,4},{6,5},{7,6},{9,8},{10,9},{11,10},{13,12},{... | collective-permute-start | bytes 392 | tf_op jit(solution)/shard_map/ppermute | solution.py:39
  233.9 7.6 %collective-permute-start.25 = (f32[32,1]{1,0:T(8,128)S(1)}, f32[32,1]{1,0:T(8,128)S(1)}, u32[]{:S(2)}, u32[]{:S(2)}) collective-permute-start(f32[32,1]{1,0:T(8,128)S(1)} %slice.461), channel_id=1, source_target_pairs={{0,1},{1,2},{2,3},{4,5},{5,6},{6,7},{8,9},{9,10},{10,11},{12,13},{... | collective-permute-start | bytes 392 | tf_op jit(solution)/shard_map/ppermute | solution.py:39
  236.1 6.0 %collective-permute-start.27 = (f32[1,256]{1,0:T(1,128)S(1)}, f32[1,256]{1,0:T(1,128)S(1)}, u32[]{:S(2)}, u32[]{:S(2)}) collective-permute-start(f32[1,256]{1,0:T(1,128)S(1)} %slice.465), channel_id=1, source_target_pairs={{0,4},{4,8},{8,12},{12,16},{16,20},{20,24},{24,28},{1,5},{5,9},{9,... | collective-permute-start | bytes 3080 | tf_op jit(solution)/shard_map/ppermute | solution.py:39
  (10 other events, 32.5 us)
where the time goes:
time: 246 us; the launch traced here: 243 us
  starting transfers between devices  79.2 us (32%)
  other arithmetic  55.7 us (23%)
  blocking collectives  37.8 us (15%)
  local copies, waits for them, and re-layouts  32.2 us (13%)
  waiting for transfers between devices  19.7 us (8%)
  matrix products  16.4 us (7%)
    ppermute x16, starting transfers between devices, passed_along(): return lax.ppermute(block, axis, route)  39.8 us
    all_to_all x1, blocking collectives, per_device(): lax.all_to_all(outgoing, ('wide', 'narrow'), split_axis=1, concat_axis=1,...  37.8 us
    ppermute x6, starting transfers between devices, with_halo(): lax.ppermute(tail, axis, [(i, (i + 1) % count) for i in range(ends)])  22.8 us
    add x1, other arithmetic, per_device(): ocean_flux = ocean_flux + weight_sum[None] * shifted  18.1 us
    another operation x3, other arithmetic  9.41 us
    mul x1, other arithmetic, momentum(): wind_gain * stress  8.38 us
    ppermute x16, waiting for transfers between devices, passed_along(): return lax.ppermute(block, axis, route)  8.08 us
    ppermute x6, starting transfers between devices, with_halo(): lax.ppermute(head, axis, [((i + 1) % count, i) for i in range(ends)])  7.73 us
  transfers between devices with their start and end apart: 30, of which 9 were waited for; matrix products, arithmetic and copies ran while one was open for 33% of the time, Pallas kernels for 0%

commit v1 on v0

v1 whole, which is shorter than its diff:
```python
import functools

import jax
import jax.numpy as jnp
from jax import lax
from jax.experimental import pallas as pl
from jax.experimental.pallas import tpu as pltpu
from jax.sharding import PartitionSpec as P

AC = 128
NSUB = 4
LANES = 128
CHUNK = 512
VMEM_BYTES = 48 * 1024 * 1024

relax_rate = 0.5
kappa_mix = 0.2
heat_gain = 0.5
gravity = 0.7
depth_mean = 0.7
wind_gain = 0.3
fresh_gain = 0.3

f32 = jnp.float32
bf16 = jnp.bfloat16
i32 = jnp.int32
MESH = pl.DeviceIdType.MESH
SIDES = ((1, 0), (-1, 0), (0, 1), (0, -1), (1, 1), (1, -1), (-1, 1), (-1, -1))
VMEM = pl.BlockSpec(memory_space=pltpu.VMEM)


def iota(shape, dim):
    return lax.broadcasted_iota(i32, shape, dim)


def place_kernel(peers, capacity, owner_ref, atm_ref, xs_ref, slot_ref):
    count = owner_ref.shape[1]
    upper = (iota((LANES, LANES), 0) < iota((LANES, LANES), 1)).astype(bf16)
    ids = iota((peers, LANES), 0)
    carry = jnp.zeros((peers, 1), f32)
    for start in range(0, count, LANES):
        owner = owner_ref[:, start : start + LANES]
        hot = (ids == owner).astype(f32)
        before = jnp.dot(hot.astype(bf16), upper, preferred_element_type=f32) + carry
        rank = jnp.sum(hot * before, axis=0, keepdims=True)
        slot_ref[:, start : start + LANES] = owner * capacity + rank.astype(i32)
        carry = carry + jnp.sum(hot, axis=1, keepdims=True)
    columns = atm_ref[...].astype(bf16)

    def step(i, _):
        begin = pl.multiple_of(i * CHUNK, CHUNK)
        selector = (iota((CHUNK, count), 0) + begin == slot_ref[...]).astype(f32).astype(bf16)
        placed = lax.dot_general(
            columns, selector, (((1,), (1,)), ((), ())), preferred_element_type=f32
        )
        xs_ref[:, pl.ds(begin, CHUNK)] = placed.astype(bf16)
        return 0

    lax.fori_loop(0, xs_ref.shape[1] // CHUNK, step, 0)


def physics_kernel(sweeps, capacity, packed_rows, ops_ref, xs_ref, fm_ref, y_ref):
    features = xs_ref.shape[0]
    tail = features - LANES
    groups = CHUNK // capacity
    initial = [xs_ref[:, g * capacity : (g + 1) * capacity].astype(f32) for g in range(groups)]
    current = list(initial)
    for sweep in range(sweeps):
        for g in range(groups):
            base = g * packed_rows
            rounded = current[g].astype(bf16)
            parts = [rounded[:LANES]]
            if sweep > 0:
                parts.append(jnp.zeros((sweep * tail, capacity), bf16))
            parts.append(rounded[LANES:])
            parts.append(jnp.zeros((LANES - (sweep + 1) * tail, capacity), bf16))
            operand = jnp.concatenate(parts, axis=0)
            head = ops_ref[base + sweep * features : base + (sweep + 1) * features, :]
            rest = ops_ref[base + sweeps * features : base + (sweeps + 1) * features, :]
            matrix = jnp.concatenate([head, rest], axis=1)
            mixed = jnp.dot(matrix, operand, preferred_element_type=f32)
            current[g] = current[g] + relax_rate * jnp.tanh(mixed)
    for g in range(groups):
        cols = slice(g * capacity, (g + 1) * capacity)
        y_ref[:features, cols] = (current[g] - initial[g]).astype(bf16)
        fluxes = jnp.dot(fm_ref[...], current[g].astype(bf16), preferred_element_type=f32)
        y_ref[features:, cols] = fluxes.astype(bf16)


def fetch_kernel(y_ref, slot_ref, atm_ref, new_ref, flux_ref):
    features = atm_ref.shape[0]
    slots = y_ref.shape[1]
    selector = (iota((slots, slot_ref.shape[1]), 0) == slot_ref[...]).astype(f32).astype(bf16)
    returned = jnp.dot(y_ref[...], selector, preferred_element_type=f32)
    new_ref[...] = atm_ref[...] + returned[:features]
    flux_ref[...] = returned[features:]


def side_device(side):
    wide, narrow = lax.axis_size("wide"), lax.axis_size("narrow")
    return (
        lax.rem(lax.axis_index("wide") + side[0] + wide, wide),
        lax.rem(lax.axis_index("narrow") + side[1] + narrow, narrow),
    )


def greet():
    barrier = pltpu.get_barrier_semaphore()
    for side in SIDES:
        pl.semaphore_signal(barrier, inc=1, device_id=side_device(side), device_id_type=MESH)
    pl.semaphore_wait(barrier, len(SIDES))


def leaving(step, size, halo):
    if step > 0:
        return pl.ds(size - halo, halo)
    return pl.ds(0, halo) if step < 0 else pl.ds(0, size)


def landing(step, size, halo):
    if step > 0:
        return pl.ds(0, halo)
    return pl.ds(halo + size, halo) if step < 0 else pl.ds(halo, size)


def edge_copies(src, dst, halo_rows, halo_cols, send_sem, recv_sem):
    rows, cols = src.shape[1], src.shape[2]
    return [
        pltpu.make_async_remote_copy(
            src_ref=src.at[:, leaving(dr, rows, halo_rows), leaving(dc, cols, halo_cols)],
            dst_ref=dst.at[:, landing(dr, rows, halo_rows), landing(dc, cols, halo_cols)],
            send_sem=send_sem.at[k],
            recv_sem=recv_sem.at[k],
            device_id=side_device((dr, dc)),
            device_id_type=MESH,
        )
        for k, (dr, dc) in enumerate(SIDES)
    ]


HR = 8
HC = 128


def turned(x, shift, axis):
    return pltpu.roll(x, shift % x.shape[axis], axis)


def static_kernel(
    src_ref, weight_ref, mask_ref, tracer_ref, height_ref, flow_ref,
    wsum_ref, planes_ref, tracer_out_ref,
    own, ext, row_out, row_in, col_out, col_in,
    send_sem, recv_sem, tsend_sem, trecv_sem,
):
    entries, rows, cols = src_ref.shape
    levels = tracer_ref.shape[0]
    own[0] = mask_ref[...].astype(f32)
    own[1] = height_ref[...]
    own[2] = flow_ref[0]
    own[3] = flow_ref[1]
    for e in range(entries):
        own[4 + e] = src_ref[e].astype(f32)
        own[4 + entries + e] = weight_ref[e]
    ext[:, HR : HR + rows, HC : HC + cols] = own[...]
    greet()
    copies = edge_copies(own, ext, HR, HC, send_sem, recv_sem)
    for copy in copies:
        copy.start()

    lane = iota((rows, LANES), 1)

    def pack(level, carry):
        first, last = carry
        field = tracer_ref[level]
        row_out[0, pl.ds(level, 1), :] = field[rows - 1 : rows, :]
        row_out[1, pl.ds(level, 1), :] = field[0:1, :]
        first = jnp.where(lane == level, field[:, 0:1], first)
        last = jnp.where(lane == level, field[:, cols - 1 : cols], last)
        return first, last

    blank = jnp.zeros((rows, LANES), f32)
    first, last = lax.fori_loop(0, levels, pack, (blank, blank))
    for spare in range(levels, row_out.shape[1]):
        for k in range(2):
            row_out[k, spare : spare + 1, :] = jnp.zeros((1, cols), f32)
    col_out[0] = last
    col_out[1] = first
    tcopies = []
    for k in range(4):
        out, into = (row_out, row_in) if k < 2 else (col_out, col_in)
        tcopies.append(
            pltpu.make_async_remote_copy(
                src_ref=out.at[k % 2],
                dst_ref=into.at[k % 2],
                send_sem=tsend_sem.at[k],
                recv_sem=trecv_sem.at[k],
                device_id=side_device(SIDES[k]),
                device_id_type=MESH,
            )
        )
    for copy in tcopies:
        copy.start()
    for copy in copies:
        copy.wait()

    wide, narrow = lax.axis_size("wide"), lax.axis_size("narrow")
    ext_rows, ext_cols = ext.shape[1], ext.shape[2]
    row = iota((ext_rows, ext_cols), 0) + (lax.axis_index("wide") * rows - HR)
    col = iota((ext_rows, ext_cols), 1) + (lax.axis_index("narrow") * cols - HC)
    inside = (row >= 0) & (row < wide * rows) & (col >= 0) & (col < narrow * cols)
    mask = jnp.where(inside, ext[0], 0.0)
    planes_ref[0] = mask
    planes_ref[1] = ext[1]
    planes_ref[2] = ext[2]
    planes_ref[3] = ext[3]

    for slab in range(0, ext_rows, 8):
        at = slice(slab, slab + 8)
        codes = [ext[4 + e, at, :] for e in range(entries)]
        weights = [ext[4 + entries + e, at, :] for e in range(entries)]
        for code in range(9):
            total = jnp.where(codes[0] == code, weights[0], 0.0)
            for e in range(1, entries):
                total = total + jnp.where(codes[e] == code, weights[e], 0.0)
            wsum_ref[code, at, :] = total

    middle = (slice(HR, HR + rows), slice(HC, HC + cols))
    k_north, k_south, k_east, k_west = [
        (kappa_mix * mask * turned(mask, shift, axis))[middle]
        for shift, axis in ((-1, 0), (1, 0), (-1, 1), (1, 1))
    ]
    for copy in tcopies:
        copy.wait()
    row = iota((rows, cols), 0)
    col = iota((rows, cols), 1)

    def diffuse(level, _):
        field = tracer_ref[level]
        here = lane == level
        south = jnp.where(row == 0, row_in[0, pl.ds(level, 1), :], turned(field, 1, 0))
        north = jnp.where(row == rows - 1, row_in[1, pl.ds(level, 1), :], turned(field, -1, 0))
        west_edge = jnp.sum(jnp.where(here, col_in[0], 0.0), axis=1, keepdims=True)
        east_edge = jnp.sum(jnp.where(here, col_in[1], 0.0), axis=1, keepdims=True)
        west = jnp.where(col == 0, west_edge, turned(field, 1, 1))
        east = jnp.where(col == cols - 1, east_edge, turned(field, -1, 1))
        tracer_out_ref[level] = field + (
            k_north * (north - field)
            + k_south * (south - field)
            + k_east * (east - field)
            + k_west * (west - field)
        )
        return 0

    lax.fori_loop(0, levels, diffuse, 0)


def barotropic_kernel(
    flux_ref, wsum_ref, planes_ref,
    heat_ref, height_ref, flow_ref,
    own, ext, spread_cols, forcing, send_sem, recv_sem,
):
    nflux, rows, cols = flux_ref.shape
    ext_rows, ext_cols = planes_ref.shape[1], planes_ref.shape[2]
    wide, narrow = lax.axis_size("wide"), lax.axis_size("narrow")
    my_wide, my_narrow = lax.axis_index("wide"), lax.axis_index("narrow")
    own[...] = flux_ref[...]
    ext[:, HR : HR + rows, HC : HC + cols] = own[...]
    greet()
    copies = edge_copies(own, ext, HR, HC, send_sem, recv_sem)
    for copy in copies:
        copy.start()

    source = iota((cols + 2 * HC, ext_cols), 0) - HC + my_narrow * cols
    half = my_narrow * cols - HC // 2 + lax.shift_right_logical(iota((cols + 2 * HC, ext_cols), 1), 1)
    for dc in range(3):
        wanted = jnp.clip(half + (dc - 1), 0, narrow * cols - 1)
        spread_cols[:, dc * ext_cols : (dc + 1) * ext_cols] = (
            (source == wanted).astype(f32).astype(bf16)
        )
    source = iota((ext_rows, rows + 2 * HR), 1) - HR + my_wide * rows
    half = my_wide * rows - HR // 2 + lax.shift_right_logical(iota((ext_rows, rows + 2 * HR), 0), 1)
    spread_rows = jnp.concatenate(
        [
            (source == jnp.clip(half + (dr - 1), 0, wide * rows - 1)).astype(f32).astype(bf16)
            for dr in range(3)
        ],
        axis=0,
    )
    for copy in copies:
        copy.wait()

    stretched = [
        jnp.dot(ext[f].astype(bf16), spread_cols[...], preferred_element_type=f32).astype(bf16)
        for f in range(nflux)
    ]
    for f in range(nflux):
        doubled = jnp.dot(spread_rows, stretched[f], preferred_element_type=f32)
        total = None
        for code in range(9):
            dr, dc = code // 3, code % 3
            part = doubled[
                dr * ext_rows : (dr + 1) * ext_rows, dc * ext_cols : (dc + 1) * ext_cols
            ]
            term = wsum_ref[code] * part
            total = term if total is None else total + term
        forcing[f] = total

    mask = planes_ref[0]
    mask_east = mask * turned(mask, -1, 1)
    mask_north = mask * turned(mask, -1, 0)
    height, flow_u, flow_v = planes_ref[1], planes_ref[2], planes_ref[3]
    fresh = fresh_gain * forcing[1]
    stress_u = wind_gain * forcing[2]
    stress_v = wind_gain * forcing[3]
    for _ in range(NSUB):
        flow_u = mask_east * (flow_u - gravity * (turned(height, -1, 1) - height) + stress_u)
        flow_v = mask_north * (flow_v - gravity * (turned(height, -1, 0) - height) + stress_v)
        spread = (flow_u - turned(flow_u, 1, 1)) + (flow_v - turned(flow_v, 1, 0))
        height = mask * (height - depth_mean * spread + fresh)
    middle = (
        slice(HR, HR + height_ref.shape[0]),
        slice(HC, HC + height_ref.shape[1]),
    )
    heat_ref[...] = (heat_gain * mask * forcing[0])[middle]
    height_ref[...] = height[middle]
    flow_ref[0] = flow_u[middle]
    flow_ref[1] = flow_v[middle]


def params(**more):
    return pltpu.CompilerParams(vmem_limit_bytes=VMEM_BYTES, **more)


def per_device(
    atm_state,
    group_owner,
    regime_ops,
    flux_map,
    remap_src,
    remap_weight,
    ocean_mask,
    tracer,
    surface_height,
    transports,
):
    peers = lax.axis_size(("wide", "narrow"))
    features, columns_here = atm_state.shape
    nflux = flux_map.shape[1]
    capacity = 2 * columns_here // peers
    total_slots = peers * capacity
    sweeps = regime_ops.shape[1]
    tail = features - LANES
    entries, rows, cols = remap_src.shape
    levels = tracer.shape[0]
    shape = jax.ShapeDtypeStruct

    turned_ops = jnp.swapaxes(regime_ops[0], 1, 2)
    heads = turned_ops[:, :, :LANES].reshape(sweeps * features, LANES)
    rests = jnp.swapaxes(turned_ops[:, :, LANES:], 0, 1).reshape(features, sweeps * tail)
    rests = jnp.pad(rests, ((0, 0), (0, LANES - sweeps * tail)))
    packed = jnp.concatenate([heads, rests], axis=0)
    packed_rows = packed.shape[0]
    gathered = lax.all_gather(packed, ("wide", "narrow"), axis=0, tiled=True)

    placed, slots = pl.pallas_call(
        functools.partial(place_kernel, peers, capacity),
        out_shape=(shape((features, total_slots), bf16), shape((1, columns_here), i32)),
        in_specs=[VMEM] * 2,
        out_specs=(VMEM,) * 2,
        compiler_params=params(),
        cost_estimate=pl.CostEstimate(
            flops=2 * features * columns_here * total_slots,
            bytes_accessed=4 * features * columns_here + 2 * features * total_slots,
            transcendentals=0,
        ),
        name="place",
    )(group_owner.reshape(1, columns_here), atm_state)

    ext_rows, ext_cols = rows + 2 * HR, cols + 2 * HC
    padded_levels = -(-levels // 8) * 8
    wsum, planes, tracer_mixed = pl.pallas_call(
        static_kernel,
        out_shape=(
            shape((9, ext_rows, ext_cols), f32),
            shape((4, ext_rows, ext_cols), f32),
            shape(tracer.shape, f32),
        ),
        in_specs=[VMEM] * 6,
        out_specs=(VMEM,) * 3,
        scratch_shapes=[
            pltpu.VMEM((4 + 2 * entries, rows, cols), f32),
            pltpu.VMEM((4 + 2 * entries, ext_rows, ext_cols), f32),
            pltpu.VMEM((2, padded_levels, cols), f32),
            pltpu.VMEM((2, padded_levels, cols), f32),
            pltpu.VMEM((2, rows, LANES), f32),
            pltpu.VMEM((2, rows, LANES), f32),
            pltpu.SemaphoreType.DMA((8,)),
            pltpu.SemaphoreType.DMA((8,)),
            pltpu.SemaphoreType.DMA((4,)),
            pltpu.SemaphoreType.DMA((4,)),
        ],
        compiler_params=params(collective_id=0, has_side_effects=True),
        cost_estimate=pl.CostEstimate(
            flops=20 * tracer.size, bytes_accessed=8 * tracer.size, transcendentals=0
        ),
        name="static",
    )(remap_src, remap_weight, ocean_mask, tracer, surface_height, transports)

    groups = CHUNK // capacity
    padded_map = jnp.pad(flux_map.T, ((0, 16 - nflux), (0, 0)))
    y_rows = features + 16
    answers = pl.pallas_call(
        functools.partial(physics_kernel, sweeps, capacity, packed_rows),
        grid=(total_slots // CHUNK,),
        out_shape=shape((y_rows, total_slots), bf16),
        in_specs=[
            pl.BlockSpec((groups * packed_rows, LANES), lambda i: (i, 0)),
            pl.BlockSpec((features, CHUNK), lambda i: (0, i)),
            pl.BlockSpec((16, features), lambda i: (0, 0)),
        ],
        out_specs=pl.BlockSpec((y_rows, CHUNK), lambda i: (0, i)),
        compiler_params=params(),
        name="physics",
    )(gathered, placed, padded_map)

    atm_new, fluxes = pl.pallas_call(
        fetch_kernel,
        grid=(columns_here // CHUNK,),
        out_shape=(shape((features, columns_here), f32), shape((16, columns_here), f32)),
        in_specs=[
            pl.BlockSpec((y_rows, total_slots), lambda i: (0, 0)),
            pl.BlockSpec((1, CHUNK), lambda i: (0, i)),
            pl.BlockSpec((features, CHUNK), lambda i: (0, i)),
        ],
        out_specs=(
            pl.BlockSpec((features, CHUNK), lambda i: (0, i)),
            pl.BlockSpec((16, CHUNK), lambda i: (0, i)),
        ),
        compiler_params=params(),
        name="fetch",
    )(answers, slots, atm_state)

    block_rows = columns_here // AC
    flux_block = fluxes[:nflux].reshape(nflux, block_rows, AC)
    heat, height, flows = pl.pallas_call(
        barotropic_kernel,
        out_shape=(
            shape((rows, cols), f32),
            shape((rows, cols), f32),
            shape((2, rows, cols), f32),
        ),
        in_specs=[VMEM] * 3,
        out_specs=(VMEM,) * 3,
        scratch_shapes=[
            pltpu.VMEM((nflux, block_rows, AC), f32),
            pltpu.VMEM((nflux, block_rows + 2 * HR, AC + 2 * HC), f32),
            pltpu.VMEM((AC + 2 * HC, 3 * ext_cols), bf16),
            pltpu.VMEM((nflux, ext_rows, ext_cols), f32),
            pltpu.SemaphoreType.DMA((8,)),
            pltpu.SemaphoreType.DMA((8,)),
        ],
        compiler_params=params(collective_id=1, has_side_effects=True),
        name="barotropic",
    )(flux_block, wsum, planes)
    tracer_new = tracer_mixed.at[0].add(heat)
    return (atm_new, tracer_new, height, flows)


def solution(mesh):
    in_specs = (
        P(None, ("wide", "narrow")),
        P(("wide", "narrow"), None),
        P(("wide", "narrow"), None, None, None),
        P(),
        P(None, "wide", "narrow"),
        P(None, "wide", "narrow"),
        P("wide", "narrow"),
        P(None, "wide", "narrow"),
        P("wide", "narrow"),
        P(None, "wide", "narrow"),
    )
    out_specs = (
        P(None, ("wide", "narrow")),
        P(None, "wide", "narrow"),
        P("wide", "narrow"),
        P(None, "wide", "narrow"),
    )
    return jax.shard_map(
        per_device, mesh=mesh, in_specs=in_specs, out_specs=out_specs, check_vma=False
    )
```

time: 246 us -> 122 us (0.50); the launches traced: 243 us -> 122 us
  starting transfers between devices: 79.2 us -> 0.04 us
  Pallas kernels: 0 us -> 56.1 us
  other arithmetic: 55.7 us -> 0.71 us
  blocking collectives: 37.8 us -> 0 us
  local copies, waits for them, and re-layouts: 32.2 us -> 13.9 us
  waiting for transfers between devices: 19.7 us -> 36.6 us
  matrix products: 16.4 us -> 0 us
  between operations: 1.92 us -> 14.1 us
    ppermute x28 -> x0, starting transfers between devices: 70.3 us -> none  [the longest x16 39.8 us: passed_along(): return lax.ppermute(block, axis, route)]
    pallas_call x0 -> x5, Pallas kernels: none -> 56.1 us  [the longest x1 25.9 us: per_device(): pl.pallas_call(static_kernel, out_shape=(shape((9, ext_rows, ext_cols), f...]
    all_to_all x1 -> x0, blocking collectives: 37.8 us -> none  [per_device(): lax.all_to_all(outgoing, ('wide', 'narrow'), split_axis=1, concat_axis=1,...]
    all_gather x0 -> x1, waiting for transfers between devices: none -> 36.6 us  [per_device(): gathered = lax.all_gather(packed, ('wide', 'narrow'), axis=0, tiled=True)]
    add x12 -> x0, other arithmetic: 24.2 us -> none  [the longest x1 18.1 us: per_device(): ocean_flux = ocean_flux + weight_sum[None] * shifted]
    dot_general x17 -> x0, matrix products: 16.4 us -> none  [the longest x8 6.97 us: place_columns(): jnp.dot(source, selector, preferred_element_type=jnp.float32)]
    mul x10 -> x0, other arithmetic: 13.3 us -> none  [the longest x1 8.38 us: momentum(): wind_gain * stress]
    slice x35 -> x3, local copies, waits for them, and re-layouts: 14.5 us -> 1.91 us  [the longest x2 1.14 us: per_device(): heads = turned_ops[:, :, :LANES].reshape(sweeps * features, LANES)]
  transfers between devices with their start and end apart: 30 -> 1, of which waited for: 9 -> 1; matrix products, arithmetic and copies ran while one was open for 33% -> 1% of each run, Pallas kernels for 0% -> 27%
where the time goes in v1:
time: 122 us
  Pallas kernels  56.1 us (46%)
  waiting for transfers between devices  36.6 us (30%)
  between operations  14.1 us (12%)
  local copies, waits for them, and re-layouts  13.9 us (11%)
    all_gather x1, waiting for transfers between devices, per_device(): gathered = lax.all_gather(packed, ('wide', 'narrow'), axis=0, tiled=True)  36.6 us
    pallas_call x1, Pallas kernels, per_device(): pl.pallas_call(static_kernel, out_shape=(shape((9, ext_rows, ext_cols), f...  25.9 us
    unnamed x31, local copies, waits for them, and re-layouts  11.2 us
    pallas_call x1, Pallas kernels, per_device(): pl.pallas_call(barotropic_kernel, out_shape=(shape((rows, cols), f32), sh...  9.58 us
    pallas_call x1, Pallas kernels, per_device(): pl.pallas_call(functools.partial(physics_kernel, sweeps, capacity, packed...  9.26 us
    pallas_call x1, Pallas kernels, per_device(): pl.pallas_call(functools.partial(place_kernel, peers, capacity), out_shap...  6.95 us
    pallas_call x1, Pallas kernels, per_device(): pl.pallas_call(fetch_kernel, grid=(columns_here // CHUNK,), out_shape=(sh...  4.38 us
  transfers between devices with their start and end apart: 1, of which 1 were waited for; matrix products, arithmetic and copies ran while one was open for 1% of the time, Pallas kernels for 27%

profile of v1, /device:TPU:0, one launch (start us, length us, event | category | flops | bytes accessed | tf_op | source)
XLA Modules:
  0.0 121.5 jit_solution(5639673100307361067)
XLA Ops:
  7.2 0.0 all-gather.2.cloned.1.call-start
  7.2 0.0 copy-start.12
  7.2 0.8 slice.36
  8.0 1.0 slice.35
  9.0 0.1 copy.17
  9.1 0.2 copy.16
  9.2 0.7 fusion.1
  9.9 0.0 all-gather.2.cloned.1.call-update
  10.0 0.7 pad.11.fm_ref
  10.7 0.0 copy-start
  10.7 1.6 %copy-done = f32[62,32,256]{2,1,0:T(8,128)S(1)} copy-done((f32[62,32,256]{2,1,0:T(8,128)S(1)}, f32[62,32,256]{2,1,0:T(8,128)}, u32[]{:S(2)}) %copy-start) | copy-done | bytes 2031640
  12.2 0.0 copy-start.7
  12.2 0.9 copy-done.7
  13.1 0.0 copy-start.8
  13.1 0.9 copy-done.8
  14.0 0.0 copy-start.9
  14.0 0.8 copy-done.9
  14.9 0.0 copy-start.10
  14.9 0.8 copy-done.10
  15.6 0.0 copy-start.11
  15.6 0.8 copy-done.11
  16.4 25.9 %static.1 = (f32[9,48,512]{2,1,0:T(8,128)S(1)}, f32[4,48,512]{2,1,0:T(8,128)S(1)}, f32[62,32,256]{2,1,0:T(8,128)S(1)}) custom-call(s32[4,32,256]{2,1,0:T(8,128)S(1)} %copy-done.7, f32[4,32,256]{2,1,0:T(8,128)S(1)} %copy-done.8, s32[32,256]{1,0:T(8,128)S(1)} %copy-done.10, f32[62,32,256]{2,1,0:T(8,128)S(1)} %copy-done, f32[32,256]{1,0:T(8,128)S(1)} %copy-done.11, ...), custom_call_target="tpu_custom_call" | custom-call | flops 10158080 | bytes 4063232 | tf_op jit(solution)/shard_map/static/pallas_call | solution.py:381
  42.3 0.0 copy-start.3
  42.3 0.9 copy-done.3
  43.2 0.0 copy-start.5
  43.2 0.8 copy-done.5
  44.0 0.0 copy-done.12
  44.0 0.0 copy-start.1
  44.0 1.3 %copy-done.1 = f32[144,2048]{1,0:T(8,128)S(1)} copy-done((f32[144,2048]{1,0:T(8,128)S(1)}, f32[144,2048]{1,0:T(8,128)}, u32[]{:S(2)}) %copy-start.1) | copy-done | bytes 1179672
  45.3 6.9 %place.1 = (bf16[144,4096]{1,0:T(8,128)(2,1)S(1)}, s32[1,2048]{1,0:T(1,128)S(1)}) custom-call(s32[1,2048]{1,0:T(1,128)S(1)} %bitcast.19, f32[144,2048]{1,0:T(8,128)S(1)} %copy-done.1), custom_call_target="tpu_custom_call" | custom-call | flops 2415919104 | bytes 2359296 | tf_op jit(solution)/shard_map/place/pallas_call | solution.py:365
  52.2 36.6 %all-gather.2.cloned.1.call-done.ops_ref = bf16[23040,128]{1,0:T(8,128)(2,1)} async-done(((bf16[720,128]{1,0:T(8,128)(2,1)}), bf16[23040,128]{1,0:T(8,128)(2,1)}) %all-gather.2.cloned.1.call-update) | async-done | bytes 5898256 | tf_op jit(solution)/shard_map/all_gather | solution.py:363
  88.8 0.0 copy-start.2
  88.9 9.3 %physics.1.y_ref = bf16[160,4096]{1,0:T(8,128)(2,1)S(1)} custom-call(bf16[23040,128]{1,0:T(8,128)(2,1)} %all-gather.2.cloned.1.call-done.ops_ref, bf16[144,4096]{1,0:T(8,128)(2,1)S(1)} %get-tuple-element.26.xs_ref, bf16[16,144]{1,0:T(8,128)(2,1)S(1)} %pad.11.fm_ref), custom_call_target="tpu_custom_call" | custom-call | tf_op jit(solution)/shard_map/physics/pallas_call | solution.py:412
  98.1 0.0 copy-start.4
  98.1 0.0 copy-start.6
  98.1 0.0 copy-done.2
  98.1 4.4 %fetch.1 = (f32[144,2048]{1,0:T(8,128)}, f32[16,2048]{1,0:T(8,128)S(1)}) custom-call(bf16[160,4096]{1,0:T(8,128)(2,1)S(1)} %physics.1.y_ref, s32[1,2048]{1,0:T(1,128)S(1)} %get-tuple-element.27.slot_ref, f32[144,2048]{1,0:T(8,128)S(1)} %copy-done.2), custom_call_target="tpu_custom_call" | custom-call | tf_op jit(solution)/shard_map/fetch/pallas_call | solution.py:426
  102.5 0.0 copy-done.4
  102.5 0.0 copy-done.6
  102.5 9.6 %barotropic.1 = (f32[32,256]{1,0:T(8,128)S(1)}, f32[32,256]{1,0:T(8,128)S(1)}, f32[2,32,256]{2,1,0:T(8,128)S(1)}) custom-call(f32[4,16,128]{2,1,0:T(8,128)S(1)} %bitcast.18, f32[9,48,512]{2,1,0:T(8,128)S(1)} %copy-done.4, f32[4,48,512]{2,1,0:T(8,128)S(1)} %copy-done.6), custom_call_target="tpu_custom_call" | custom-call | tf_op jit(solution)/shard_map/barotropic/pallas_call | solution.py:445
  112.1 1.3 %copy.25 = f32[62,32,256]{2,1,0:T(8,128)} copy(f32[62,32,256]{2,1,0:T(8,128)S(1)} %fusion.2) | data formatting | bytes 4063232
  113.4 0.6 copy.26
  114.1 0.6 copy.27
  (3 shorter events, 0.0 us)
Async XLA Ops:
  7.2 81.7 %all-gather.2.cloned.1.call-start = ((), (), s32[]{:S(2)}) async-start(), calls=%async_computation | async-start | bytes 6082560 | tf_op jit(solution)/shard_map/all_gather | solution.py:363
  7.2 36.8 %copy-start.12 = (s32[2048,1]{0,1:T(1,128)S(1)}, s32[2048,1]{0,1:T(1,128)}, u32[]{:S(2)}) copy-start(s32[2048,1]{0,1:T(1,128)} %param.13) | copy-start | bytes 24580
  10.7 1.6 %copy-start = (f32[62,32,256]{2,1,0:T(8,128)S(1)}, f32[62,32,256]{2,1,0:T(8,128)}, u32[]{:S(2)}) copy-start(f32[62,32,256]{2,1,0:T(8,128)} %tracer_ref.1) | copy-start | bytes 6094852
  12.2 0.9 copy-start.7
  13.1 0.9 copy-start.8
  14.0 0.8 copy-start.9
  14.9 0.8 copy-start.10
  15.6 0.8 copy-start.11
  42.3 0.9 copy-start.3
  43.2 0.8 copy-start.5
  44.0 1.3 %copy-start.1 = (f32[144,2048]{1,0:T(8,128)S(1)}, f32[144,2048]{1,0:T(8,128)}, u32[]{:S(2)}) copy-start(f32[144,2048]{1,0:T(8,128)} %atm_ref.3) | copy-start | bytes 3538948
  88.8 9.3 %copy-start.2 = (f32[144,2048]{1,0:T(8,128)S(1)}, f32[144,2048]{1,0:T(8,128)}, u32[]{:S(2)}) copy-start(f32[144,2048]{1,0:T(8,128)} %atm_ref.3) | copy-start | bytes 3538948
  98.1 4.4 %copy-start.4 = (f32[9,48,512]{2,1,0:T(8,128)S(1)}, f32[9,48,512]{2,1,0:T(8,128)}, u32[]{:S(2)}) copy-start(f32[9,48,512]{2,1,0:T(8,128)} %copy-done.3) | copy-start | bytes 2654212
  98.1 4.4 %copy-start.6 = (f32[4,48,512]{2,1,0:T(8,128)S(1)}, f32[4,48,512]{2,1,0:T(8,128)}, u32[]{:S(2)}) copy-start(f32[4,48,512]{2,1,0:T(8,128)} %copy-done.5) | copy-start | bytes 1179652
Sparse Core Ops, SparseCore 0:
  11.5 77.3 all-gather.1

commit v2 on v1

--- a/solution.py
+++ b/solution.py
@@ -8,6 +8,7 @@
 from jax.sharding import PartitionSpec as P
 
 AC = 128
+PHYS = 512
 NSUB = 4
 LANES = 128
 CHUNK = 512
@@ -33,36 +34,10 @@
     return lax.broadcasted_iota(i32, shape, dim)
 
 
-def place_kernel(peers, capacity, owner_ref, atm_ref, xs_ref, slot_ref):
-    count = owner_ref.shape[1]
-    upper = (iota((LANES, LANES), 0) < iota((LANES, LANES), 1)).astype(bf16)
-    ids = iota((peers, LANES), 0)
-    carry = jnp.zeros((peers, 1), f32)
-    for start in range(0, count, LANES):
-        owner = owner_ref[:, start : start + LANES]
-        hot = (ids == owner).astype(f32)
-        before = jnp.dot(hot.astype(bf16), upper, preferred_element_type=f32) + carry
-        rank = jnp.sum(hot * before, axis=0, keepdims=True)
-        slot_ref[:, start : start + LANES] = owner * capacity + rank.astype(i32)
-        carry = carry + jnp.sum(hot, axis=1, keepdims=True)
-    columns = atm_ref[...].astype(bf16)
-
-    def step(i, _):
-        begin = pl.multiple_of(i * CHUNK, CHUNK)
-        selector = (iota((CHUNK, count), 0) + begin == slot_ref[...]).astype(f32).astype(bf16)
-        placed = lax.dot_general(
-            columns, selector, (((1,), (1,)), ((), ())), preferred_element_type=f32
-        )
-        xs_ref[:, pl.ds(begin, CHUNK)] = placed.astype(bf16)
-        return 0
-
-    lax.fori_loop(0, xs_ref.shape[1] // CHUNK, step, 0)
-
-
 def physics_kernel(sweeps, capacity, packed_rows, ops_ref, xs_ref, fm_ref, y_ref):
     features = xs_ref.shape[0]
     tail = features - LANES
-    groups = CHUNK // capacity
+    groups = PHYS // capacity
     initial = [xs_ref[:, g * capacity : (g + 1) * capacity].astype(f32) for g in range(groups)]
     current = list(initial)
     for sweep in range(sweeps):
@@ -104,11 +79,11 @@
     )
 
 
-def greet():
+def greet(sides=SIDES):
     barrier = pltpu.get_barrier_semaphore()
-    for side in SIDES:
+    for side in sides:
         pl.semaphore_signal(barrier, inc=1, device_id=side_device(side), device_id_type=MESH)
-    pl.semaphore_wait(barrier, len(SIDES))
+    pl.semaphore_wait(barrier, len(sides))
 
 
 def leaving(step, size, halo):
@@ -146,14 +121,121 @@
     return pltpu.roll(x, shift % x.shape[axis], axis)
 
 
-def static_kernel(
-    src_ref, weight_ref, mask_ref, tracer_ref, height_ref, flow_ref,
-    wsum_ref, planes_ref, tracer_out_ref,
-    own, ext, row_out, row_in, col_out, col_in,
-    send_sem, recv_sem, tsend_sem, trecv_sem,
+class Gather:
+    def __init__(self, packed, slots, send_sem, recv_sem):
+        self.packed, self.slots = packed, slots
+        self.send_sem, self.recv_sem = send_sem, recv_sem
+        wide, self.narrow = lax.axis_size("wide"), lax.axis_size("narrow")
+        self.zs = wide // 2
+        w, n = lax.axis_index("wide"), lax.axis_index("narrow")
+        self.z, self.y, self.x, self.c = w // 2, lax.rem(w, 2), n // 2, lax.rem(n, 2)
+        self.offsets = [0]
+        for d in range(1, self.zs // 2 + 1):
+            self.offsets += [-d, d] if d < self.zs - d else [-d]
+        self.sent = {}
+
+    def index(self, kind, k):
+        z = lax.rem(self.z + self.offsets[k] + self.zs, self.zs)
+        y = 1 - self.y if kind in "yd" else self.y
+        x = 1 - self.x if kind in "xd" else self.x
+        return (z * 2 + y) * self.narrow + x * 2 + self.c
+
+    def place(self, way):
+        z = lax.rem(self.z + way.get("z", 0) + self.zs, self.zs)
+        y = 1 - self.y if "y" in way else self.y
+        x = 1 - self.x if "x" in way else self.x
+        c = 1 - self.c if "c" in way else self.c
+        return z * 2 + y, x * 2 + c
+
+    def number(self, kind, k):
+        if kind[0] == "c":
+            return 4 * self.zs + self.number(kind[1], k)
+        return "zxyd".index(kind) * self.zs + k
+
+    def send(self, have, k, kind, to, way):
+        at = self.index(have, k)
+        event = self.number(kind, to)
+        copy = pltpu.make_async_remote_copy(
+            src_ref=self.packed if have == "z" and k == 0 else self.slots.at[at],
+            dst_ref=self.slots.at[at],
+            send_sem=self.send_sem.at[event],
+            recv_sem=self.recv_sem.at[event],
+            device_id=self.place(way),
+            device_id_type=MESH,
+        )
+        copy.start()
+        self.sent[kind, to] = copy
+
+    def onward(self, kind, k):
+        if kind == "z":
+            d = self.offsets[k]
+            if d <= 0 and d - 1 in self.offsets:
+                self.send("z", k, "z", self.offsets.index(d - 1), {"z": 1})
+            if d >= 0 and d + 1 in self.offsets:
+                self.send("z", k, "z", self.offsets.index(d + 1), {"z": -1})
+            self.send("z", k, "x", k, {"x": 1})
+            self.send("z", k, "y", k, {"y": 1})
+        elif kind == "x" and k % 2 == 0:
+            self.send("x", k, "d", k, {"y": 1})
+        elif kind == "y" and k % 2 == 1:
+            self.send("y", k, "d", k, {"x": 1})
+        self.send(kind, k, "c" + kind, k, {"c": 1})
+
+    def arrive(self, kind, k):
+        self.sent[kind, k].wait_recv()
+        if kind[0] != "c":
+            self.onward(kind, k)
+
+    def rounds(self):
+        steps = []
+        for k in range(self.zs):
+            if k > 0:
+                steps.append([("z", k)])
+                steps.append([("x", k - 1), ("y", k - 1)])
+        steps.append([("x", self.zs - 1), ("y", self.zs - 1)])
+        for k in range(self.zs):
+            steps.append([("d", k)])
+        return steps
+
+
+AROUND = SIDES + ((2, 0), (-2, 0), (0, 2))
+
+
+def prepare_kernel(
+    capacity,
+    packed_hbm, owner_ref, atm_hbm, src_hbm, weight_hbm, mask_hbm, tracer_hbm, height_hbm, flow_hbm,
+    slots_hbm, xs_ref, slot_ref, wsum_ref, planes_ref, tracer_out_ref,
+    atm_ref, src_ref, weight_ref, mask_ref, tracer_ref, height_ref, flow_ref,
+    own, ext, row_out, row_in, col_out, col_in, coef,
+    gsend_sem, grecv_sem, load_sem, send_sem, recv_sem, tsend_sem, trecv_sem,
 ):
     entries, rows, cols = src_ref.shape
     levels = tracer_ref.shape[0]
+    wide, narrow = lax.axis_size("wide"), lax.axis_size("narrow")
+    peers = wide * narrow
+    gather = Gather(packed_hbm, slots_hbm, gsend_sem, grecv_sem)
+    loads = [
+        pltpu.make_async_copy(a, b, load_sem.at[k])
+        for k, (a, b) in enumerate(
+            (
+                (mask_hbm, mask_ref),
+                (height_hbm, height_ref),
+                (flow_hbm, flow_ref),
+                (src_hbm, src_ref),
+                (weight_hbm, weight_ref),
+                (tracer_hbm, tracer_ref),
+                (atm_hbm, atm_ref),
+                (packed_hbm, slots_hbm.at[gather.index("z", 0)]),
+            )
+        )
+    ]
+    for load in loads:
+        load.start()
+    greet(AROUND)
+    gather.onward("z", 0)
+
+    for load in loads[:5]:
+        load.wait()
     own[0] = mask_ref[...].astype(f32)
     own[1] = height_ref[...]
     own[2] = flow_ref[0]
@@ -162,10 +244,10 @@
         own[4 + e] = src_ref[e].astype(f32)
         own[4 + entries + e] = weight_ref[e]
     ext[:, HR : HR + rows, HC : HC + cols] = own[...]
-    greet()
     copies = edge_copies(own, ext, HR, HC, send_sem, recv_sem)
     for copy in copies:
         copy.start()
+    loads[5].wait()
 
     lane = iota((rows, LANES), 1)
 
@@ -200,37 +282,64 @@
         )
     for copy in tcopies:
         copy.start()
-    for copy in copies:
-        copy.wait()
-
-    wide, narrow = lax.axis_size("wide"), lax.axis_size("narrow")
+
+    def rank():
+        loads[6].wait()
+        loads[7].wait()
+        count = owner_ref.shape[1]
+        upper = (iota((LANES, LANES), 0) < iota((LANES, LANES), 1)).astype(f32).astype(bf16)
+        ids = iota((peers, LANES), 0)
+        carry = jnp.zeros((peers, 1), f32)
+        for start in range(0, count, LANES):
+            owner = owner_ref[:, start : start + LANES]
+            hot = (ids == owner).astype(f32)
+            before = jnp.dot(hot.astype(bf16), upper, preferred_element_type=f32) + carry
+            ranks = jnp.sum(hot * before, axis=0, keepdims=True)
+            slot_ref[:, start : start + LANES] = owner * capacity + ranks.astype(i32)
+            carry = carry + jnp.sum(hot, axis=1, keepdims=True)
+
+    def place(first, last):
+        columns = atm_ref[...].astype(bf16)
+
+        def step(i, _):
+            begin = pl.multiple_of(i * CHUNK, CHUNK)
+            selector = (iota((CHUNK, slot_ref.shape[1]), 0) + begin == slot_ref[...]).astype(f32)
+            placed = lax.dot_general(
+                columns, selector.astype(bf16), (((1,), (1,)), ((), ())), preferred_element_type=f32
+            )
+            xs_ref[:, pl.ds(begin, CHUNK)] = placed.astype(bf16)
+            return 0
+
+        lax.fori_loop(first, last, step, 0)
+
+    middle = (slice(HR, HR + rows), slice(HC, HC + cols))
     ext_rows, ext_cols = ext.shape[1], ext.shape[2]
-    row = iota((ext_rows, ext_cols), 0) + (lax.axis_index("wide") * rows - HR)
-    col = iota((ext_rows, ext_cols), 1) + (lax.axis_index("narrow") * cols - HC)
-    inside = (row >= 0) & (row < wide * rows) & (col >= 0) & (col < narrow * cols)
-    mask = jnp.where(inside, ext[0], 0.0)
-    planes_ref[0] = mask
-    planes_ref[1] = ext[1]
-    planes_ref[2] = ext[2]
-    planes_ref[3] = ext[3]
-
-    for slab in range(0, ext_rows, 8):
-        at = slice(slab, slab + 8)
-        codes = [ext[4 + e, at, :] for e in range(entries)]
-        weights = [ext[4 + entries + e, at, :] for e in range(entries)]
-        for code in range(9):
-            total = jnp.where(codes[0] == code, weights[0], 0.0)
-            for e in range(1, entries):
-                total = total + jnp.where(codes[e] == code, weights[e], 0.0)
-            wsum_ref[code, at, :] = total
-
-    middle = (slice(HR, HR + rows), slice(HC, HC + cols))
-    k_north, k_south, k_east, k_west = [
-        (kappa_mix * mask * turned(mask, shift, axis))[middle]
-        for shift, axis in ((-1, 0), (1, 0), (-1, 1), (1, 1))
-    ]
-    for copy in tcopies:
-        copy.wait()
+
+    def planes():
+        for copy in copies:
+            copy.wait()
+        row = iota((ext_rows, ext_cols), 0) + (lax.axis_index("wide") * rows - HR)
+        col = iota((ext_rows, ext_cols), 1) + (lax.axis_index("narrow") * cols - HC)
+        inside = (row >= 0) & (row < wide * rows) & (col >= 0) & (col < narrow * cols)
+        mask = jnp.where(inside, ext[0], 0.0)
+        planes_ref[0] = mask
+        planes_ref[1] = ext[1]
+        planes_ref[2] = ext[2]
+        planes_ref[3] = ext[3]
+        for k, (shift, axis) in enumerate(((-1, 0), (1, 0), (-1, 1), (1, 1))):
+            coef[k] = (kappa_mix * mask * turned(mask, shift, axis))[middle]
+
+    def weights(first, last):
+        for slab in range(first, last, 8):
+            at = slice(slab, slab + 8)
+            codes = [ext[4 + e, at, :] for e in range(entries)]
+            parts = [ext[4 + entries + e, at, :] for e in range(entries)]
+            for code in range(9):
+                total = jnp.where(codes[0] == code, parts[0], 0.0)
+                for e in range(1, entries):
+                    total = total + jnp.where(codes[e] == code, parts[e], 0.0)
+                wsum_ref[code, at, :] = total
+
     row = iota((rows, cols), 0)
     col = iota((rows, cols), 1)
 
@@ -244,14 +353,37 @@
         west = jnp.where(col == 0, west_edge, turned(field, 1, 1))
         east = jnp.where(col == cols - 1, east_edge, turned(field, -1, 1))
         tracer_out_ref[level] = field + (
-            k_north * (north - field)
-            + k_south * (south - field)
-            + k_east * (east - field)
-            + k_west * (west - field)
+            coef[0] * (north - field)
+            + coef[1] * (south - field)
+            + coef[2] * (east - field)
+            + coef[3] * (west - field)
         )
         return 0
 
-    lax.fori_loop(0, levels, diffuse, 0)
+    def mix(first, last):
+        if first == 0:
+            for copy in tcopies:
+                copy.wait()
+        lax.fori_loop(first, last, diffuse, 0)
+
+    chunks = xs_ref.shape[1] // CHUNK
+    work = [rank]
+    work += [functools.partial(place, i, min(i + 2, chunks)) for i in range(0, chunks, 2)]
+    work += [planes]
+    work += [functools.partial(weights, i, i + 16) for i in range(0, ext_rows, 16)]
+    work += [functools.partial(mix, i, min(i + 16, levels)) for i in range(0, levels, 16)]
+    for events in gather.rounds():
+        if work:
+            work.pop(0)()
+        for event in events:
+            gather.arrive(*event)
+    while work:
+        work.pop(0)()
+    for kind in "zxyd":
+        for k in range(gather.zs):
+            gather.arrive("c" + kind, k)
+    for copy in gather.sent.values():
+        copy.wait_send()
 
 
 def barotropic_kernel(
@@ -360,40 +492,40 @@
     rests = jnp.pad(rests, ((0, 0), (0, LANES - sweeps * tail)))
     packed = jnp.concatenate([heads, rests], axis=0)
     packed_rows = packed.shape[0]
-    gathered = lax.all_gather(packed, ("wide", "narrow"), axis=0, tiled=True)
-
-    placed, slots = pl.pallas_call(
-        functools.partial(place_kernel, peers, capacity),
-        out_shape=(shape((features, total_slots), bf16), shape((1, columns_here), i32)),
-        in_specs=[VMEM] * 2,
-        out_specs=(VMEM,) * 2,
-        compiler_params=params(),
-        cost_estimate=pl.CostEstimate(
-            flops=2 * features * columns_here * total_slots,
-            bytes_accessed=4 * features * columns_here + 2 * features * total_slots,
-            transcendentals=0,
-        ),
-        name="place",
-    )(group_owner.reshape(1, columns_here), atm_state)
-
     ext_rows, ext_cols = rows + 2 * HR, cols + 2 * HC
     padded_levels = -(-levels // 8) * 8
-    wsum, planes, tracer_mixed = pl.pallas_call(
-        static_kernel,
+    gather_events = 8 * (lax.axis_size("wide") // 2)
+    hbm = pl.BlockSpec(memory_space=pl.ANY)
+    gathered, placed, slots, wsum, planes, tracer_mixed = pl.pallas_call(
+        functools.partial(prepare_kernel, capacity),
         out_shape=(
+            shape((peers,) + packed.shape, bf16),
+            shape((features, total_slots), bf16),
+            shape((1, columns_here), i32),
             shape((9, ext_rows, ext_cols), f32),
             shape((4, ext_rows, ext_cols), f32),
             shape(tracer.shape, f32),
         ),
-        in_specs=[VMEM] * 6,
-        out_specs=(VMEM,) * 3,
+        in_specs=[hbm, VMEM] + [hbm] * 7,
+        out_specs=(hbm,) + (VMEM,) * 5,
         scratch_shapes=[
+            pltpu.VMEM(atm_state.shape, f32),
+            pltpu.VMEM(remap_src.shape, i32),
+            pltpu.VMEM(remap_weight.shape, f32),
+            pltpu.VMEM(ocean_mask.shape, i32),
+            pltpu.VMEM(tracer.shape, f32),
+            pltpu.VMEM(surface_height.shape, f32),
+            pltpu.VMEM(transports.shape, f32),
             pltpu.VMEM((4 + 2 * entries, rows, cols), f32),
             pltpu.VMEM((4 + 2 * entries, ext_rows, ext_cols), f32),
             pltpu.VMEM((2, padded_levels, cols), f32),
             pltpu.VMEM((2, padded_levels, cols), f32),
             pltpu.VMEM((2, rows, LANES), f32),
             pltpu.VMEM((2, rows, LANES), f32),
+            pltpu.VMEM((4, rows, cols), f32),
+            pltpu.SemaphoreType.DMA((gather_events,)),
+            pltpu.SemaphoreType.DMA((gather_events,)),
+            pltpu.SemaphoreType.DMA((8,)),
             pltpu.SemaphoreType.DMA((8,)),
             pltpu.SemaphoreType.DMA((8,)),
             pltpu.SemaphoreType.DMA((4,)),
@@ -401,24 +533,37 @@
         ],
         compiler_params=params(collective_id=0, has_side_effects=True),
         cost_estimate=pl.CostEstimate(
-            flops=20 * tracer.size, bytes_accessed=8 * tracer.size, transcendentals=0
+            flops=2 * features * columns_here * total_slots,
+            bytes_accessed=8 * tracer.size,
+            transcendentals=0,
         ),
-        name="static",
-    )(remap_src, remap_weight, ocean_mask, tracer, surface_height, transports)
-
-    groups = CHUNK // capacity
+        name="prepare",
+    )(
+        packed,
+        group_owner.reshape(1, columns_here),
+        atm_state,
+        remap_src,
+        remap_weight,
+        ocean_mask,
+        tracer,
+        surface_height,
+        transports,
+    )
+    gathered = gathered.reshape(peers * packed_rows, LANES)
+
+    groups = PHYS // capacity
     padded_map = jnp.pad(flux_map.T, ((0, 16 - nflux), (0, 0)))
     y_rows = features + 16
     answers = pl.pallas_call(
         functools.partial(physics_kernel, sweeps, capacity, packed_rows),
-        grid=(total_slots // CHUNK,),
+        grid=(total_slots // PHYS,),
         out_shape=shape((y_rows, total_slots), bf16),
         in_specs=[
             pl.BlockSpec((groups * packed_rows, LANES), lambda i: (i, 0)),
-            pl.BlockSpec((features, CHUNK), lambda i: (0, i)),
+            pl.BlockSpec((features, PHYS), lambda i: (0, i)),
             pl.BlockSpec((16, features), lambda i: (0, 0)),
         ],
-        out_specs=pl.BlockSpec((y_rows, CHUNK), lambda i: (0, i)),
+        out_specs=pl.BlockSpec((y_rows, PHYS), lambda i: (0, i)),
         compiler_params=params(),
         name="physics",
     )(gathered, placed, padded_map)

time: 122 us -> 86.8 us (0.71)
  waiting for transfers between devices: 36.6 us -> 0 us
  Pallas kernels: 56.1 us -> 73.9 us
  between operations: 14.1 us -> 0.71 us
  local copies, waits for them, and re-layouts: 13.9 us -> 11.4 us
    all_gather x1 -> x0, waiting for transfers between devices: 36.6 us -> none  [per_device(): gathered = lax.all_gather(packed, ('wide', 'narrow'), axis=0, tiled=True)]
    pallas_call x2 -> x1, Pallas kernels: 32.9 us -> 50.8 us  [per_device(): pl.pallas_call(functools.partial(prepare_kernel, capacity), out_shape=(sh...]
    unnamed x31 -> x23, local copies, waits for them, and re-layouts: 11.2 us -> 8.68 us
  transfers between devices with their start and end apart: 1 -> 0, of which waited for: 1 -> 0; matrix products, arithmetic and copies ran while one was open for 1% -> 0% of each run, Pallas kernels for 27% -> 0%
where the time goes in v2:
time: 86.8 us; the launch traced here: 86.1 us
  Pallas kernels  73.9 us (85%)
  local copies, waits for them, and re-layouts  11.4 us (13%)
    pallas_call x1, Pallas kernels, per_device(): pl.pallas_call(functools.partial(prepare_kernel, capacity), out_shape=(sh...  50.8 us
    pallas_call x1, Pallas kernels, per_device(): pl.pallas_call(barotropic_kernel, out_shape=(shape((rows, cols), f32), sh...  9.52 us
    pallas_call x1, Pallas kernels, per_device(): pl.pallas_call(functools.partial(physics_kernel, sweeps, capacity, packed...  9.28 us
    unnamed x23, local copies, waits for them, and re-layouts  8.68 us
    pallas_call x1, Pallas kernels, per_device(): pl.pallas_call(fetch_kernel, grid=(columns_here // CHUNK,), out_shape=(sh...  4.38 us

profile of v2, /device:TPU:0, one launch (start us, length us, event | category | flops | bytes accessed | tf_op | source)
XLA Modules:
  0.0 86.1 jit_solution(1940416729076898323)
XLA Ops:
  0.6 0.7 pad.11.fm_ref
  1.3 0.8 slice.36
  2.1 0.1 copy.17
  2.2 1.0 %slice.35 = bf16[4,144,128]{1,2,0:T(8,128)(2,1)S(1)} slice(bf16[4,144,144]{1,2,0:T(8,128)(2,1)} %bitcast.24), slice={[0:4], [0:144], [0:128]} | slice | bytes 294912 | tf_op jit(solution)/shard_map/slice | solution.py:490
  3.2 0.2 copy.16
  3.4 0.0 copy-start
  3.4 1.3 %copy-done = f32[144,2048]{1,0:T(8,128)S(1)} copy-done((f32[144,2048]{1,0:T(8,128)S(1)}, f32[144,2048]{1,0:T(8,128)}, u32[]{:S(2)}) %copy-start) | copy-done | bytes 1179672
  4.6 0.0 copy-start.2
  4.6 0.9 %copy-done.2 = s32[4,32,256]{2,1,0:T(8,128)S(1)} copy-done((s32[4,32,256]{2,1,0:T(8,128)S(1)}, s32[4,32,256]{2,1,0:T(8,128)}, u32[]{:S(2)}) %copy-start.2) | copy-done | bytes 131096
  5.5 0.0 copy-start.3
  5.5 0.9 %copy-done.3 = f32[4,32,256]{2,1,0:T(8,128)S(1)} copy-done((f32[4,32,256]{2,1,0:T(8,128)S(1)}, f32[4,32,256]{2,1,0:T(8,128)}, u32[]{:S(2)}) %copy-start.3) | copy-done | bytes 131096
  6.5 0.0 copy-start.4
  6.5 0.8 copy-done.4
  7.3 0.0 copy-start.5
  7.3 0.8 copy-done.5
  8.1 0.0 copy-start.6
  8.1 0.8 copy-done.6
  8.8 0.0 copy-start.7
  8.8 0.7 copy-done.7
  9.5 50.8 %prepare.1 = (bf16[32,720,128]{2,1,0:T(8,128)(2,1)}, bf16[144,4096]{1,0:T(8,128)(2,1)S(1)}, s32[1,2048]{1,0:T(1,128)S(1)}, f32[9,48,512]{2,1,0:T(8,128)S(1)}, f3...) custom-call(bf16[720,128]{1,0:T(8,128)(2,1)S(1)} %fusion.1.packed_hbm, s32[1,2048]{1,0:T(1,128)S(1)} %bitcast.20, ...), custom_call_target="tpu_custom_call" | custom-call | flops 2415919104 | bytes 4063232 | tf_op jit(solution)/shard_map/prepare/pallas_call | solution.py:499
  60.3 0.0 copy-start.1
  60.3 9.3 %physics.1.y_ref = bf16[160,4096]{1,0:T(8,128)(2,1)S(1)} custom-call(bf16[23040,128]{1,0:T(8,128)(2,1)} %bitcast.21, bf16[144,4096]{1,0:T(8,128)(2,1)S(1)} %get-tuple-element.28.xs_ref, bf16[16,144]{1,0:T(8,128)(2,1)S(1)} %pad.11.fm_ref), custom_call_target="tpu_custom_call" | custom-call | tf_op jit(solution)/shard_map/physics/pallas_call | solution.py:557
  69.6 0.0 copy-done.1
  69.6 0.0 copy-start.8
  69.6 4.4 %fetch.1 = (f32[144,2048]{1,0:T(8,128)}, f32[16,2048]{1,0:T(8,128)S(1)}) custom-call(bf16[160,4096]{1,0:T(8,128)(2,1)S(1)} %physics.1.y_ref, s32[1,2048]{1,0:T(1,128)S(1)} %get-tuple-element.29.slot_ref, f32[144,2048]{1,0:T(8,128)S(1)} %copy-done.1), custom_call_target="tpu_custom_call" | custom-call | tf_op jit(solution)/shard_map/fetch/pallas_call | solution.py:571
  74.0 9.5 %barotropic.1 = (f32[32,256]{1,0:T(8,128)S(1)}, f32[32,256]{1,0:T(8,128)S(1)}, f32[2,32,256]{2,1,0:T(8,128)S(1)}) custom-call(f32[4,16,128]{2,1,0:T(8,128)S(1)} %bitcast.19, f32[9,48,512]{2,1,0:T(8,128)S(1)} %get-tuple-element.33.wsum_ref, f32[4,48,512]{2,1,0:T(8,128)S(1)} %get-tuple-element.34.planes_ref), custom_call_target="tpu_custom_call" | custom-call | tf_op jit(solution)/shard_map/barotropic/pallas_call | solution.py:590
  83.5 0.0 copy-done.8
  83.5 1.3 %copy.25 = f32[62,32,256]{2,1,0:T(8,128)} copy(f32[62,32,256]{2,1,0:T(8,128)S(1)} %fusion.2) | data formatting | bytes 4063232
  84.8 0.6 copy.26
  85.4 0.6 copy.27
  (4 shorter events, 0.0 us)
Async XLA Ops:
  3.4 1.3 %copy-start = (f32[144,2048]{1,0:T(8,128)S(1)}, f32[144,2048]{1,0:T(8,128)}, u32[]{:S(2)}) copy-start(f32[144,2048]{1,0:T(8,128)} %atm_ref.1) | copy-start | bytes 3538948
  4.6 0.9 %copy-start.2 = (s32[4,32,256]{2,1,0:T(8,128)S(1)}, s32[4,32,256]{2,1,0:T(8,128)}, u32[]{:S(2)}) copy-start(s32[4,32,256]{2,1,0:T(8,128)} %src_hbm.1) | copy-start | bytes 393220
  5.5 0.9 %copy-start.3 = (f32[4,32,256]{2,1,0:T(8,128)S(1)}, f32[4,32,256]{2,1,0:T(8,128)}, u32[]{:S(2)}) copy-start(f32[4,32,256]{2,1,0:T(8,128)} %weight_hbm.1) | copy-start | bytes 393220
  6.5 0.8 copy-start.4
  7.3 0.8 copy-start.5
  8.1 0.8 copy-start.6
  8.8 0.7 copy-start.7
  60.3 9.3 %copy-start.1 = (f32[144,2048]{1,0:T(8,128)S(1)}, f32[144,2048]{1,0:T(8,128)}, u32[]{:S(2)}) copy-start(f32[144,2048]{1,0:T(8,128)} %atm_ref.1) | copy-start | bytes 3538948
  69.6 13.9 %copy-start.8 = (f32[62,32,256]{2,1,0:T(8,128)S(1)}, f32[62,32,256]{2,1,0:T(8,128)}, u32[]{:S(2)}) copy-start(f32[62,32,256]{2,1,0:T(8,128)} %get-tuple-element.31) | copy-start | bytes 6094852

commit v3 on v2

--- a/solution.py
+++ b/solution.py
@@ -13,6 +13,7 @@
 LANES = 128
 CHUNK = 512
 VMEM_BYTES = 48 * 1024 * 1024
+ALL_VMEM_BYTES = 60 * 1024 * 1024
 
 relax_rate = 0.5
 kappa_mix = 0.2
@@ -459,8 +460,8 @@
     flow_ref[1] = flow_v[middle]
 
 
-def params(**more):
-    return pltpu.CompilerParams(vmem_limit_bytes=VMEM_BYTES, **more)
+def params(limit=VMEM_BYTES, **more):
+    return pltpu.CompilerParams(vmem_limit_bytes=limit, **more)
 
 
 def per_device(
@@ -531,7 +532,7 @@
             pltpu.SemaphoreType.DMA((4,)),
             pltpu.SemaphoreType.DMA((4,)),
         ],
-        compiler_params=params(collective_id=0, has_side_effects=True),
+        compiler_params=params(limit=ALL_VMEM_BYTES, collective_id=0, has_side_effects=True),
         cost_estimate=pl.CostEstimate(
             flops=2 * features * columns_here * total_slots,
             bytes_accessed=8 * tracer.size,

time: 86.8 us -> 83.4 us (0.961)
  local copies, waits for them, and re-layouts: 11.4 us -> 6.53 us
  Pallas kernels: 73.9 us -> 74.9 us
    unnamed x23 -> x17, local copies, waits for them, and re-layouts: 8.68 us -> 3.83 us
    pallas_call x1, Pallas kernels: 50.8 us -> 51.8 us  [per_device(): pl.pallas_call(functools.partial(prepare_kernel, capacity), out_shape=(sh...]
where the time goes in v3:
time: 83.4 us; the launch traced here: 82.9 us
  Pallas kernels  74.9 us (90%)
  local copies, waits for them, and re-layouts  6.53 us (8%)
    pallas_call x1, Pallas kernels, per_device(): pl.pallas_call(functools.partial(prepare_kernel, capacity), out_shape=(sh...  51.8 us
    pallas_call x1, Pallas kernels, per_device(): pl.pallas_call(barotropic_kernel, out_shape=(shape((rows, cols), f32), sh...  9.51 us
    pallas_call x1, Pallas kernels, per_device(): pl.pallas_call(functools.partial(physics_kernel, sweeps, capacity, packed...  9.26 us
    pallas_call x1, Pallas kernels, per_device(): pl.pallas_call(fetch_kernel, grid=(columns_here // CHUNK,), out_shape=(sh...  4.38 us
    unnamed x17, local copies, waits for them, and re-layouts  3.83 us

profile of v3, /device:TPU:0, one launch (start us, length us, event | category | flops | bytes accessed | tf_op | source)
XLA Modules:
  0.0 82.9 jit_solution(14617054734859000683)
XLA Ops:
  0.6 0.7 pad.11.fm_ref
  1.3 0.8 slice.36
  2.1 0.1 copy.17
  2.2 1.0 %slice.35 = bf16[4,144,128]{1,2,0:T(8,128)(2,1)S(1)} slice(bf16[4,144,144]{1,2,0:T(8,128)(2,1)} %bitcast.23), slice={[0:4], [0:144], [0:128]} | slice | bytes 294912 | tf_op jit(solution)/shard_map/slice | solution.py:491
  3.2 0.2 copy.16
  3.3 0.7 fusion.1.packed_hbm
  4.0 51.8 %prepare.1 = (bf16[32,720,128]{2,1,0:T(8,128)(2,1)}, bf16[144,4096]{1,0:T(8,128)(2,1)}, s32[1,2048]{1,0:T(1,128)}, f32[9,48,512]{2,1,0:T(8,128)}, f32[4,48,512]{2,1,0:T(8,128)}, /*index=5*/f32[62,32,256]{2,1,0:T(8,128)}) custom-call(bf16[720,128]{1,0:T(8,128)(2,1)} %fusion.1.packed_hbm, s32[1,2048]{1,0:T(1,128)} %bitcast.26, f32[144,2048]{1,0:T(8,128)} %atm_ref.1, ...), custom_call_target="tpu_custom_call" | custom-call | flops 2415919104 | bytes 4063232 | tf_op jit(solution)/shard_map/prepare/pallas_call | solution.py:500
  55.8 0.0 copy-start
  55.9 1.3 %copy-done = bf16[144,4096]{1,0:T(8,128)(2,1)S(1)} copy-done((bf16[144,4096]{1,0:T(8,128)(2,1)S(1)}, bf16[144,4096]{1,0:T(8,128)(2,1)}, u32[]{:S(2)}) %copy-start) | copy-done | bytes 1179672
  57.1 0.0 copy-start.1
  57.1 0.0 copy-start.4
  57.1 9.3 %physics.1.y_ref = bf16[160,4096]{1,0:T(8,128)(2,1)S(1)} custom-call(bf16[23040,128]{1,0:T(8,128)(2,1)} %bitcast.20, bf16[144,4096]{1,0:T(8,128)(2,1)S(1)} %copy-done, bf16[16,144]{1,0:T(8,128)(2,1)S(1)} %pad.11.fm_ref), custom_call_target="tpu_custom_call" | custom-call | tf_op jit(solution)/shard_map/physics/pallas_call | solution.py:558
  66.4 0.0 copy-done.1
  66.4 0.0 copy-done.4
  66.4 0.0 copy-start.2
  66.4 0.0 copy-start.3
  66.4 0.0 copy-start.5
  66.4 4.4 %fetch.1 = (f32[144,2048]{1,0:T(8,128)}, f32[16,2048]{1,0:T(8,128)S(1)}) custom-call(bf16[160,4096]{1,0:T(8,128)(2,1)S(1)} %physics.1.y_ref, s32[1,2048]{1,0:T(1,128)S(1)} %copy-done.4, f32[144,2048]{1,0:T(8,128)S(1)} %copy-done.1), custom_call_target="tpu_custom_call" | custom-call | tf_op jit(solution)/shard_map/fetch/pallas_call | solution.py:572
  70.8 0.0 copy-done.2
  70.8 0.0 copy-done.3
  70.8 9.5 %barotropic.1 = (f32[32,256]{1,0:T(8,128)S(1)}, f32[32,256]{1,0:T(8,128)S(1)}, f32[2,32,256]{2,1,0:T(8,128)S(1)}) custom-call(f32[4,16,128]{2,1,0:T(8,128)S(1)} %bitcast.19, f32[9,48,512]{2,1,0:T(8,128)S(1)} %copy-done.2, f32[4,48,512]{2,1,0:T(8,128)S(1)} %copy-done.3), custom_call_target="tpu_custom_call" | custom-call | tf_op jit(solution)/shard_map/barotropic/pallas_call | solution.py:591
  80.3 0.0 copy-done.5
  80.4 1.3 %copy.25 = f32[62,32,256]{2,1,0:T(8,128)} copy(f32[62,32,256]{2,1,0:T(8,128)S(1)} %fusion.2) | data formatting | bytes 4063232
  81.7 0.6 copy.26
  82.3 0.6 copy.27
  (3 shorter events, 0.0 us)
Async XLA Ops:
  55.8 1.3 %copy-start = (bf16[144,4096]{1,0:T(8,128)(2,1)S(1)}, bf16[144,4096]{1,0:T(8,128)(2,1)}, u32[]{:S(2)}) copy-start(bf16[144,4096]{1,0:T(8,128)(2,1)} %get-tuple-element.28.xs_ref) | copy-start | bytes 3538948
  57.1 9.3 %copy-start.1 = (f32[144,2048]{1,0:T(8,128)S(1)}, f32[144,2048]{1,0:T(8,128)}, u32[]{:S(2)}) copy-start(f32[144,2048]{1,0:T(8,128)} %atm_ref.1) | copy-start | bytes 3538948
  57.1 9.3 %copy-start.4 = (s32[1,2048]{1,0:T(1,128)S(1)}, s32[1,2048]{1,0:T(1,128)}, u32[]{:S(2)}) copy-start(s32[1,2048]{1,0:T(1,128)} %get-tuple-element.29.slot_ref) | copy-start | bytes 24580
  66.4 4.4 %copy-start.2 = (f32[9,48,512]{2,1,0:T(8,128)S(1)}, f32[9,48,512]{2,1,0:T(8,128)}, u32[]{:S(2)}) copy-start(f32[9,48,512]{2,1,0:T(8,128)} %get-tuple-element.33.wsum_ref) | copy-start | bytes 2654212
  66.4 4.4 %copy-start.3 = (f32[4,48,512]{2,1,0:T(8,128)S(1)}, f32[4,48,512]{2,1,0:T(8,128)}, u32[]{:S(2)}) copy-start(f32[4,48,512]{2,1,0:T(8,128)} %get-tuple-element.34.planes_ref) | copy-start | bytes 1179652
  66.4 13.9 %copy-start.5 = (f32[62,32,256]{2,1,0:T(8,128)S(1)}, f32[62,32,256]{2,1,0:T(8,128)}, u32[]{:S(2)}) copy-start(f32[62,32,256]{2,1,0:T(8,128)} %get-tuple-element.31) | copy-start | bytes 6094852

commit v4 on v3

--- a/solution.py
+++ b/solution.py
@@ -8,7 +8,7 @@
 from jax.sharding import PartitionSpec as P
 
 AC = 128
-PHYS = 512
+PHYS = 1024
 NSUB = 4
 LANES = 128
 CHUNK = 512

time: 83.4 us -> 79.8 us (0.957)
  Pallas kernels: 74.9 us -> 71.4 us
    pallas_call x1, Pallas kernels: 9.26 us -> 5.77 us  [per_device(): pl.pallas_call(functools.partial(physics_kernel, sweeps, capacity, packed...]
where the time goes in v4:
time: 79.8 us; the launch traced here: 79.4 us
  Pallas kernels  71.4 us (89%)
  local copies, waits for them, and re-layouts  6.53 us (8%)
    pallas_call x1, Pallas kernels, per_device(): pl.pallas_call(functools.partial(prepare_kernel, capacity), out_shape=(sh...  51.8 us
    pallas_call x1, Pallas kernels, per_device(): pl.pallas_call(barotropic_kernel, out_shape=(shape((rows, cols), f32), sh...  9.5 us
    pallas_call x1, Pallas kernels, per_device(): pl.pallas_call(functools.partial(physics_kernel, sweeps, capacity, packed...  5.77 us
    pallas_call x1, Pallas kernels, per_device(): pl.pallas_call(fetch_kernel, grid=(columns_here // CHUNK,), out_shape=(sh...  4.37 us
    unnamed x17, local copies, waits for them, and re-layouts  3.83 us

profile of v4, /device:TPU:0, one launch (start us, length us, event | category | flops | bytes accessed | tf_op | source)
XLA Modules:
  0.0 79.4 jit_solution(7211658389264047111)
XLA Ops:
  0.6 0.7 pad.11.fm_ref
  1.3 0.8 slice.36
  2.1 0.1 copy.17
  2.2 1.0 %slice.35 = bf16[4,144,128]{1,2,0:T(8,128)(2,1)S(1)} slice(bf16[4,144,144]{1,2,0:T(8,128)(2,1)} %bitcast.23), slice={[0:4], [0:144], [0:128]} | slice | bytes 294912 | tf_op jit(solution)/shard_map/slice | solution.py:491
  3.2 0.2 copy.16
  3.3 0.7 fusion.1.packed_hbm
  4.0 51.8 %prepare.1 = (bf16[32,720,128]{2,1,0:T(8,128)(2,1)}, bf16[144,4096]{1,0:T(8,128)(2,1)}, s32[1,2048]{1,0:T(1,128)}, f32[9,48,512]{2,1,0:T(8,128)}, f32[4,48,512]{2,1,0:T(8,128)}, /*index=5*/f32[62,32,256]{2,1,0:T(8,128)}) custom-call(bf16[720,128]{1,0:T(8,128)(2,1)} %fusion.1.packed_hbm, s32[1,2048]{1,0:T(1,128)} %bitcast.26, f32[144,2048]{1,0:T(8,128)} %atm_ref.1, ...), custom_call_target="tpu_custom_call" | custom-call | flops 2415919104 | bytes 4063232 | tf_op jit(solution)/shard_map/prepare/pallas_call | solution.py:500
  55.8 0.0 copy-start
  55.9 1.3 %copy-done = bf16[144,4096]{1,0:T(8,128)(2,1)S(1)} copy-done((bf16[144,4096]{1,0:T(8,128)(2,1)S(1)}, bf16[144,4096]{1,0:T(8,128)(2,1)}, u32[]{:S(2)}) %copy-start) | copy-done | bytes 1179672
  57.1 0.0 copy-start.1
  57.1 0.0 copy-start.4
  57.1 5.8 %physics.1.y_ref = bf16[160,4096]{1,0:T(8,128)(2,1)S(1)} custom-call(bf16[23040,128]{1,0:T(8,128)(2,1)} %bitcast.20, bf16[144,4096]{1,0:T(8,128)(2,1)S(1)} %copy-done, bf16[16,144]{1,0:T(8,128)(2,1)S(1)} %pad.11.fm_ref), custom_call_target="tpu_custom_call" | custom-call | tf_op jit(solution)/shard_map/physics/pallas_call | solution.py:558
  62.9 0.0 copy-done.1
  62.9 0.0 copy-done.4
  62.9 0.0 copy-start.2
  62.9 0.0 copy-start.3
  62.9 0.0 copy-start.5
  62.9 4.4 %fetch.1 = (f32[144,2048]{1,0:T(8,128)}, f32[16,2048]{1,0:T(8,128)S(1)}) custom-call(bf16[160,4096]{1,0:T(8,128)(2,1)S(1)} %physics.1.y_ref, s32[1,2048]{1,0:T(1,128)S(1)} %copy-done.4, f32[144,2048]{1,0:T(8,128)S(1)} %copy-done.1), custom_call_target="tpu_custom_call" | custom-call | tf_op jit(solution)/shard_map/fetch/pallas_call | solution.py:572
  67.3 0.0 copy-done.2
  67.3 0.0 copy-done.3
  67.3 9.5 %barotropic.1 = (f32[32,256]{1,0:T(8,128)S(1)}, f32[32,256]{1,0:T(8,128)S(1)}, f32[2,32,256]{2,1,0:T(8,128)S(1)}) custom-call(f32[4,16,128]{2,1,0:T(8,128)S(1)} %bitcast.19, f32[9,48,512]{2,1,0:T(8,128)S(1)} %copy-done.2, f32[4,48,512]{2,1,0:T(8,128)S(1)} %copy-done.3), custom_call_target="tpu_custom_call" | custom-call | tf_op jit(solution)/shard_map/barotropic/pallas_call | solution.py:591
  76.9 0.0 copy-done.5
  76.9 1.3 %copy.25 = f32[62,32,256]{2,1,0:T(8,128)} copy(f32[62,32,256]{2,1,0:T(8,128)S(1)} %fusion.2) | data formatting | bytes 4063232
  78.2 0.6 copy.26
  78.8 0.6 copy.27
  (3 shorter events, 0.0 us)
Async XLA Ops:
  55.8 1.3 %copy-start = (bf16[144,4096]{1,0:T(8,128)(2,1)S(1)}, bf16[144,4096]{1,0:T(8,128)(2,1)}, u32[]{:S(2)}) copy-start(bf16[144,4096]{1,0:T(8,128)(2,1)} %get-tuple-element.28.xs_ref) | copy-start | bytes 3538948
  57.1 5.8 %copy-start.1 = (f32[144,2048]{1,0:T(8,128)S(1)}, f32[144,2048]{1,0:T(8,128)}, u32[]{:S(2)}) copy-start(f32[144,2048]{1,0:T(8,128)} %atm_ref.1) | copy-start | bytes 3538948
  57.1 5.8 %copy-start.4 = (s32[1,2048]{1,0:T(1,128)S(1)}, s32[1,2048]{1,0:T(1,128)}, u32[]{:S(2)}) copy-start(s32[1,2048]{1,0:T(1,128)} %get-tuple-element.29.slot_ref) | copy-start | bytes 24580
  62.9 4.4 %copy-start.2 = (f32[9,48,512]{2,1,0:T(8,128)S(1)}, f32[9,48,512]{2,1,0:T(8,128)}, u32[]{:S(2)}) copy-start(f32[9,48,512]{2,1,0:T(8,128)} %get-tuple-element.33.wsum_ref) | copy-start | bytes 2654212
  62.9 4.4 %copy-start.3 = (f32[4,48,512]{2,1,0:T(8,128)S(1)}, f32[4,48,512]{2,1,0:T(8,128)}, u32[]{:S(2)}) copy-start(f32[4,48,512]{2,1,0:T(8,128)} %get-tuple-element.34.planes_ref) | copy-start | bytes 1179652
  62.9 13.9 %copy-start.5 = (f32[62,32,256]{2,1,0:T(8,128)S(1)}, f32[62,32,256]{2,1,0:T(8,128)}, u32[]{:S(2)}) copy-start(f32[62,32,256]{2,1,0:T(8,128)} %get-tuple-element.31) | copy-start | bytes 6094852
